TPU v7x, 256 devices: a whole 4x4x8 slice. The times are simulated.
256 devices in a mesh: dp: 16 (over y, z_lo, core), space: 4 (over x), tensor: 4 (over z_hi).
Axes of the slice: x: 4, y: 4, z: 8 (z_hi: 4, z_lo: 2; z = z_hi * 2 + z_lo), core: 2. Of those that a mesh axis runs over, the one named last changes fastest.
Arguments:
- tokens: bfloat16 [16, 1024, 4096], P('dp', 'space'), may hold values from -4 to 4
- weights: bfloat16 [4096, 3, 2048], P('dp', None, 'tensor'), may hold values from -0.0625 to 0.0625
- cotangent: bfloat16 [16, 1024, 2048], P('dp', 'space', 'tensor'), may hold values from -6 to 6
Outputs:
- attended: bfloat16 [16, 1024, 2048], P('dp', 'space', 'tensor')
- token_grad: bfloat16 [16, 1024, 4096], P('dp', 'space', 'tensor')
- weight_grad: float32 [4096, 3, 2048], P('dp', None, 'tensor')
All inputs are finite; a program needn't handle non-finite values.
Results may differ from a plain program's by a relative error of at most 0.039.
Values may be sent and summed in bfloat16 or wider, within the bound.
No kernel may reach another device: no remote copies, remote signals or barrier semaphores. Data moves between devices by JAX's collectives and lax.ppermute only.
A program may use at most 128 MiB of HBM per device.

v0:
```python
import functools
import math

import jax
import jax.numpy as jnp
from jax import lax
from jax.experimental import pallas as pl
from jax.experimental.pallas import tpu as pltpu
from jax.sharding import Mesh
from jax.sharding import PartitionSpec as P

HS = 128
CORE, X, T, Y, Z = range(5)
BF = jnp.bfloat16
BUSY = 2 * 10**10
F32 = jnp.float32
PARAMS = pltpu.CompilerParams(vmem_limit_bytes=60 * 1024 * 1024)
SMALL = pltpu.CompilerParams(vmem_limit_bytes=24 * 1024 * 1024)


def dot(a, b, ca, cb):
    return lax.dot_general(a, b, (((ca,), (cb,)), ((), ())), preferred_element_type=F32)


def cost(flops, nbytes, exps=0):
    return pl.CostEstimate(flops=flops, bytes_accessed=nbytes, transcendentals=exps)


def shape(*dims, dtype=BF):
    return jax.ShapeDtypeStruct(dims, dtype)


def unit_kernel(at_ref, tok_ref, root_ref, *refs, band):
    tok = tok_ref[...].astype(F32)
    root = jnp.sqrt(jnp.mean(tok * tok, -1, keepdims=True) + 1e-05)
    root_ref[...] = root
    core = at_ref[CORE]
    mine_ref, mine_t_ref = refs[:2]
    for i in range(mine_ref.shape[1] // band):
        span = slice(i * band, (i + 1) * band)
        for ref, which in zip((mine_ref, *refs[2:]), (core, 1 - core)):
            at = pl.multiple_of((2 * i + which) * band, band)
            unit = (tok_ref[:, pl.ds(at, band)].astype(F32) / root).astype(BF)
            ref[:, span] = unit
            if ref is mine_ref:
                mine_t_ref[0, span, :] = unit.T


def unit_rows(ids, tokens, band, both):
    rows, width = tokens.shape
    tile = 128
    half = width // 2
    row = pl.BlockSpec((tile, half), lambda i, at: (i, 0))
    return pl.pallas_call(
        functools.partial(unit_kernel, band=band),
        grid_spec=pltpu.PrefetchScalarGridSpec(
            num_scalar_prefetch=1,
            grid=(rows // tile,),
            in_specs=[pl.BlockSpec((tile, width), lambda i, at: (i, 0))],
            out_specs=(pl.BlockSpec((tile, 1), lambda i, at: (i, 0)), row)
            + (pl.BlockSpec((1, half, tile), lambda i, at: (0, 0, i)),)
            + (row,) * both,
        ),
        out_shape=(shape(rows, 1, dtype=F32), shape(rows, half), shape(1, half, rows))
        + (shape(rows, half),) * both,
        compiler_params=PARAMS,
        cost_estimate=cost(BUSY, 1),
    )(ids, tokens)


def project_kernel(offsets, n_sums, at_ref, mine_ref, theirs_ref, *refs):
    keep_ref, give_ref, stack_ref, sems = refs[-4:]
    n = len(offsets)
    shards, sums = refs[:n], refs[n : n + n_sums]
    copies = [pltpu.make_async_copy(w, stack_ref.at[i], sems.at[i]) for i, w in enumerate(shards)]
    for copy in copies:
        copy.start()
    kinds, depth, cols = shards[0].shape
    bands = [
        pl.ds(pl.multiple_of(place_of(at_ref, *offset) * depth, depth), depth) for offset in offsets
    ]
    for i, (rows, out) in enumerate(((mine_ref, keep_ref), (theirs_ref, give_ref))):
        for j in range(kinds):
            span = slice(j * cols, (j + 1) * cols)
            total = sums[i][:, span] if n_sums else None
            for band, shard in zip(bands, shards):
                part = jnp.dot(rows[:, band], shard[j], preferred_element_type=F32)
                total = part if total is None else total + part
            out[:, span] = total.astype(out.dtype)
    for copy in copies:
        copy.wait()


def place_of(at_ref, y, z):
    return lax.rem(at_ref[Y] + y, 4) * 2 + lax.rem(at_ref[Z] + z, 2)


def project(ids, mine, theirs, shards, offsets, sums=(), give=F32, after=()):
    rows, _ = mine.shape
    n = len(shards)
    vmem = pl.BlockSpec(memory_space=pltpu.VMEM)
    cols = 3 * shards[0].shape[-1]
    return pl.pallas_call(
        functools.partial(project_kernel, offsets, len(sums)),
        in_specs=[pl.BlockSpec(memory_space=pltpu.SMEM)]
        + [vmem] * (2 + n + len(sums))
        + [pl.BlockSpec(memory_space=pl.ANY)] * len(after),
        out_specs=(vmem, vmem, pl.BlockSpec(memory_space=pl.ANY)),
        out_shape=(
            shape(rows, cols, dtype=F32),
            shape(rows, cols, dtype=give),
            shape(n, *shards[0].shape),
        ),
        scratch_shapes=[pltpu.SemaphoreType.DMA((n,))],
        compiler_params=PARAMS,
        cost_estimate=cost(1, 1),
    )(ids, mine, theirs, *shards, *sums, *after)


def project_last_kernel(offset, carried, at_ref, mine_ref, given_ref, keep_ref, came_ref, cot_ref, *refs):
    shards, heads_ref = refs[:6], refs[-1 - carried]
    depth, cols = shards[0].shape[-2:]
    band = pl.ds(pl.multiple_of(place_of(at_ref, *offset) * depth, depth), depth)
    heads = range(heads_ref.shape[0])
    for j in range(3):
        span = slice(j * cols, (j + 1) * cols)
        total = keep_ref[:, span] + came_ref[:, span].astype(F32)
        total += jnp.dot(mine_ref[:, band], shards[j][0], preferred_element_type=F32)
        total += jnp.dot(given_ref[:, band], shards[3 + j][0], preferred_element_type=F32)
        for h in heads:
            heads_ref[h, :, j * HS : (j + 1) * HS] = total[:, h * HS : (h + 1) * HS].astype(BF)
    for h in heads:
        heads_ref[h, :, 3 * HS :] = cot_ref[:, h * HS : (h + 1) * HS]


def project_last(ids, mine, given, keep, came, cotangent, pieces, offset, heads, carry, after):
    rows, cols = keep.shape
    n = len(carry)
    vmem = pl.BlockSpec(memory_space=pltpu.VMEM)
    free = pl.BlockSpec(memory_space=pl.ANY)
    return pl.pallas_call(
        functools.partial(project_last_kernel, offset, n),
        in_specs=[pl.BlockSpec(memory_space=pltpu.SMEM)]
        + [vmem] * (5 + len(pieces))
        + [free] * (n + len(after)),
        out_specs=(vmem,) + (free,) * n,
        out_shape=(shape(heads, rows, cols // heads + HS),) + tuple(shape(*c.shape) for c in carry),
        input_output_aliases={6 + len(pieces) + i: 1 + i for i in range(n)},
        compiler_params=PARAMS,
        cost_estimate=cost(1, 1),
    )(ids, mine, given, keep, came, cotangent, *pieces, *carry, *after)


def attention_kernel(q_rows, qkv_ref, *refs):
    att_ref, grad_ref, dk_ref, dv_ref = refs[-4:]
    scale = 1.0 / math.sqrt(HS)
    key = qkv_ref[:, HS : 2 * HS]
    value = qkv_ref[:, 2 * HS : 3 * HS]
    key_t = key.T
    value_t = value.T
    for i in range(qkv_ref.shape[0] // q_rows):
        rows = pl.ds(i * q_rows, q_rows)
        query = qkv_ref[rows, 0:HS]
        dout = qkv_ref[rows, 3 * HS :]
        scores = dot(key, query, 1, 1)
        to_log2 = scale * math.log2(math.e)
        top = jnp.max(scores, axis=0, keepdims=True) * to_log2
        expo = jnp.exp2(scores * to_log2 - top)
        prob = expo * (1.0 / jnp.sum(expo, axis=0, keepdims=True))
        prob_bf = prob.astype(BF)
        att = dot(value_t, prob_bf, 1, 0).T.astype(BF)
        att_ref[rows, :] = att
        row_dot = jnp.sum((dout.astype(F32) * att.astype(F32)).T, axis=0, keepdims=True)
        dprob = dot(value, dout, 1, 1)
        dscore = (prob * (dprob - row_dot)).astype(BF)
        grad_ref[rows, 0:HS] = (dot(key_t, dscore, 1, 0) * scale).T.astype(BF)
        dv = dot(prob_bf, dout, 1, 0)
        dk = dot(dscore, query, 1, 0)
        if i == 0:
            dv_ref[...] = dv
            dk_ref[...] = dk
        else:
            dv_ref[...] += dv
            dk_ref[...] += dk
    grad_ref[:, HS : 2 * HS] = (dk_ref[...] * scale).astype(BF)
    grad_ref[:, 2 * HS : 3 * HS] = dv_ref[...].astype(BF)


def attention(qkv, after):
    n = qkv.shape[0]
    vmem = pl.BlockSpec(memory_space=pltpu.VMEM)
    return pl.pallas_call(
        functools.partial(attention_kernel, n),
        out_shape=(shape(n, HS), shape(n, 3 * HS)),
        in_specs=[vmem] + [pl.BlockSpec(memory_space=pl.ANY)] * len(after),
        out_specs=(vmem,) * 2,
        scratch_shapes=[pltpu.VMEM((n, HS), F32), pltpu.VMEM((n, HS), F32)],
        compiler_params=PARAMS,
        cost_estimate=cost(BUSY, 1),
    )(qkv, *after)


def write_stat(ref, at, stat):
    ref[at:, :] = jnp.zeros((ref.shape[0] - at, ref.shape[1]), BF)
    rest = stat
    for i in range(3):
        top = rest.astype(BF)
        ref[at + i : at + i + 1, :] = top
        rest = rest - top.astype(F32)


def read_stat(ref, at):
    return sum(ref[at + i : at + i + 1, :].astype(F32) for i in range(3))


def norm_kernel(width, halves, spots, places, n_in, at_ref, g_ref, p_ref, *refs):
    shards = refs[:n_in]
    n_out = max(spot[0] for spot in spots) + 1
    outs, stat_ref = refs[-4 - n_out : -4], refs[-4]
    w_ref, flat_ref, sems = refs[-3:]
    _, kinds, depth, cols = w_ref.shape
    band = depth // 2
    quarters = len(places) // 2

    def copy(step, core, j, source):
        to = lax.rem(at_ref[CORE] + core, 2)
        at = pl.ds(pl.multiple_of(to * band, band), band)
        return pltpu.make_async_copy(source, w_ref.at[step, j, at], sems.at[step, core, j])

    for step, (by, half) in enumerate(halves):
        y_off = lax.rem(at_ref[T] + (by + quarters) - at_ref[Y], quarters)
        where = y_off * 2 + lax.rem(at_ref[Z] + half, 2)
        for place, cores in enumerate(places):

            @pl.when(where == place)
            def _(step=step, cores=cores):
                for core, pieces in enumerate(cores):
                    for j, (which, at) in enumerate(pieces):
                        copy(step, core, j, shards[which].at[*at]).start()

    heads, _, _ = g_ref.shape
    for h in range(heads):
        for j in range(kinds):
            at = (j * heads + h) * HS
            flat_ref[at : at + HS, :] = g_ref[h, :, j * HS : (j + 1) * HS].T
    total = sum(
        g_ref[h, :, j * HS : (j + 1) * HS].astype(F32)
        * p_ref[h, :, j * HS : (j + 1) * HS].astype(F32)
        for h in range(heads)
        for j in range(kinds)
    )
    stat = jnp.sum(total.T, axis=0, keepdims=True) * (1.0 / width)
    stat_ref[...] = stat
    for ref in outs:
        if ref.shape[0] % 128:
            write_stat(ref, ref.shape[0] - 16, stat)

    for step, (which, at) in enumerate(spots):
        for core in range(2):
            for j in range(kinds):
                copy(step, core, j, shards[0].at[0]).wait()
        total = sum(
            dot(w_ref[step, j], flat_ref[j * cols : (j + 1) * cols, :], 1, 0)
            for j in range(kinds)
        )
        outs[which][at : at + depth, :] = total.astype(BF)


def norm_halves(ids, grads, proj, shards, places, halves, spots, sizes, width, after=()):
    heads, rows, _ = grads.shape
    kinds = 3
    band, cols = shards[0].shape[-2:]
    n = len(spots)
    sizes = (*sizes, 1)
    vmem = pl.BlockSpec(memory_space=pltpu.VMEM)
    free = pl.BlockSpec(memory_space=pl.ANY)
    return pl.pallas_call(
        functools.partial(norm_kernel, width, halves, spots, places, len(shards)),
        in_specs=[pl.BlockSpec(memory_space=pltpu.SMEM), vmem, vmem]
        + [free] * (len(shards) + len(after)),
        out_specs=(vmem,) * len(sizes),
        out_shape=tuple(shape(s, rows) for s in sizes[:-1]) + (shape(1, rows, dtype=F32),),
        scratch_shapes=[
            pltpu.VMEM((n, kinds, 2 * band, cols), BF),
            pltpu.VMEM((kinds * cols, rows), BF),
            pltpu.SemaphoreType.DMA((n, 2, kinds)),
        ],
        compiler_params=PARAMS,
        cost_estimate=cost(1, 1),
    )(ids, grads, proj, *shards, *after)


def add_kernel(up_part, up_in, stat_in, down_part, down_in, stat_ref, *refs):
    up_out, down_out = refs[-2:]
    half = up_part.shape[0]
    for part, came, out in ((up_part, up_in, up_out), (down_part, down_in, down_out)):
        out[:half, :] = (part[...].astype(F32) + came[...].astype(F32)).astype(BF)
    write_stat(up_out, half, stat_ref[...] + read_stat(stat_in, 0))
    write_stat(down_out, half, stat_ref[...])


def add_messages(up_part, up_in, down_part, down_in, stat, after=()):
    half, rows = up_part.shape
    block = pl.BlockSpec((half, rows), lambda i: (0, 0))
    out = pl.BlockSpec((half + 16, rows), lambda i: (0, 0))
    end = pl.BlockSpec((16, rows), lambda i: (2 * half // 16, 0))
    return pl.pallas_call(
        add_kernel,
        grid=(1,),
        out_shape=(shape(half + 16, rows),) * 2,
        in_specs=[block, block, end, block, block, pl.BlockSpec((1, rows), lambda i: (0, 0))]
        + [pl.BlockSpec(memory_space=pl.ANY)] * len(after),
        out_specs=(out, out),
        compiler_params=PARAMS,
        cost_estimate=cost(1, 1),
    )(up_part, up_in, up_in, down_part, down_in, stat, *after)


def finish_kernel(at_ref, own0, own1, up0, up1, down0, down1, tok_ref, root_ref, stat_ref, *refs):
    out_ref = refs[-1]
    half = own0.shape[0]
    stat = stat_ref[...] + read_stat(up0, half) + read_stat(down1, half)
    stat = jnp.broadcast_to(stat, (HS, stat.shape[1])).T[:, 0:1]
    root = root_ref[...]
    parts = (
        (own0[...], up0[:half, :], down0[half : 2 * half, :]),
        (own1[...], up1[half : 2 * half, :], down1[:half, :]),
    )
    for i, part in enumerate(parts):
        span = slice(i * half, (i + 1) * half)
        total = sum(p.astype(F32) for p in part)
        unit = tok_ref[:, span].astype(F32) / root
        out_ref[:, span] = ((total.T - unit * stat) / root).astype(BF)


def finish(ids, parts, tokens, root, stat, after=()):
    half, rows = parts[0].shape
    share = 2 * half
    tile = HS
    some = lambda a: pl.BlockSpec((a.shape[0], tile), lambda i, at: (0, i))
    return pl.pallas_call(
        finish_kernel,
        grid_spec=pltpu.PrefetchScalarGridSpec(
            num_scalar_prefetch=1,
            grid=(rows // tile,),
            in_specs=[some(p) for p in parts]
            + [pl.BlockSpec((tile, share), lambda i, at: (i, at[T]))]
            + [pl.BlockSpec((tile, 1), lambda i, at: (i, 0)), some(stat)]
            + [pl.BlockSpec(memory_space=pl.ANY)] * len(after),
            out_specs=pl.BlockSpec((tile, share), lambda i, at: (i, 0)),
        ),
        out_shape=shape(rows, share),
        compiler_params=PARAMS,
        cost_estimate=cost(BUSY, 1),
    )(ids, *parts, tokens, root, stat, *after)


def outer_kernel(tile, spots, at_ref, *refs):
    out_ref, a_ref, g_ref, sems = refs[-4:]
    m = max(spot[0] for spot in spots) + 1
    arrays, (mine_ref, other_ref) = refs[:m], refs[m : m + 2]
    n, rows, _ = mine_ref.shape
    depth = a_ref.shape[0]
    copies = []
    for step in range(depth // tile):
        span = pl.ds(step * tile, tile)
        some = []
        for i, (which, at, _, _) in enumerate(spots):
            to = a_ref.at[span, pl.ds(i * rows, rows)]
            some.append(pltpu.make_async_copy(arrays[which].at[at, span], to, sems.at[step, i]))
            some[-1].start()
        copies.append(some)
    for i, (_, _, by, frame) in enumerate(spots):
        ref = other_ref if frame else mine_ref
        g_ref[i * rows : (i + 1) * rows, :] = ref[lax.rem(at_ref[X] + by, n)]
    for step, some in enumerate(copies):
        for copy in some:
            copy.wait()
        span = slice(step * tile, (step + 1) * tile)
        out_ref[span, :] = jnp.dot(
            a_ref[span, :], g_ref[...], preferred_element_type=F32
        ).astype(BF)


def outer(ids, arrays, spots, mine, other, after):
    _, depth, rows = arrays[0].shape
    cols = mine.shape[2]
    n = len(spots)
    tile = 512
    vmem = pl.BlockSpec(memory_space=pltpu.VMEM)
    return pl.pallas_call(
        functools.partial(outer_kernel, tile, spots),
        in_specs=[pl.BlockSpec(memory_space=pltpu.SMEM)]
        + [pl.BlockSpec(memory_space=pl.ANY)] * len(arrays)
        + [vmem, vmem]
        + [pl.BlockSpec(memory_space=pl.ANY)] * len(after),
        out_specs=vmem,
        out_shape=shape(depth, cols),
        scratch_shapes=[
            pltpu.VMEM((depth, n * rows), BF),
            pltpu.VMEM((n * rows, cols), BF),
            pltpu.SemaphoreType.DMA((depth // tile, n)),
        ],
        compiler_params=PARAMS,
        cost_estimate=cost(1, 1),
    )(ids, *arrays, mine, other, *after)


def split_kernel(at_ref, part_ref, *refs):
    keep_ref, give_ref = refs[-2:]
    n, _, rows, _ = part_ref.shape
    for ref, which in ((keep_ref, at_ref[Z]), (give_ref, 1 - at_ref[Z])):
        ref[...] = sum(part_ref[i, which].astype(F32) for i in range(n)).astype(ref.dtype)


def split(ids, part, after=()):
    _, _, rows, cols = part.shape
    vmem = pl.BlockSpec(memory_space=pltpu.VMEM)
    return pl.pallas_call(
        split_kernel,
        in_specs=[pl.BlockSpec(memory_space=pltpu.SMEM), vmem]
        + [pl.BlockSpec(memory_space=pl.ANY)] * len(after),
        out_specs=(vmem, vmem),
        out_shape=(shape(rows, cols, dtype=F32), shape(rows, cols)),
        compiler_params=PARAMS,
        cost_estimate=cost(1, 1),
    )(ids, part, *after)


def merge_kernel(keep_ref, came_ref, att_ref, *refs):
    out_ref = refs[-1]
    total = (keep_ref[...] + came_ref[...].astype(F32)).astype(BF)
    cols = total.shape[1]
    for i in range(out_ref.shape[0]):
        out_ref[i, :, :cols] = total
        out_ref[i, :, cols:] = att_ref[i]


def merge(keep, came, att, after=()):
    rows, cols = keep.shape
    n, _, more = att.shape
    vmem = pl.BlockSpec(memory_space=pltpu.VMEM)
    return pl.pallas_call(
        merge_kernel,
        out_shape=shape(n, rows, cols + more),
        in_specs=[vmem] * 3 + [pl.BlockSpec(memory_space=pl.ANY)] * len(after),
        out_specs=vmem,
        compiler_params=PARAMS,
        cost_estimate=cost(1, 1),
    )(keep, came, att, *after)


def unpack_kernel(in_ref, w_ref, att_ref):
    for h in range(in_ref.shape[0]):
        span = slice(h * HS, (h + 1) * HS)
        for j in range(3):
            w_ref[j, :, span] = in_ref[h, :, j * HS : (j + 1) * HS].astype(F32)
        att_ref[:, span] = in_ref[h, :, 3 * HS :]


def unpack(last):
    heads, rows, more = last.shape
    tile = rows // 4
    return pl.pallas_call(
        unpack_kernel,
        grid=(rows // tile,),
        in_specs=[pl.BlockSpec((heads, tile, more), lambda i: (0, i, 0))],
        out_specs=(
            pl.BlockSpec((3, tile, heads * HS), lambda i: (0, i, 0)),
            pl.BlockSpec((tile, heads * HS), lambda i: (i, 0)),
        ),
        out_shape=(shape(3, rows, heads * HS, dtype=F32), shape(rows, heads * HS)),
        compiler_params=SMALL,
        cost_estimate=cost(1, 1),
    )(last)


def gate(arrays, after=(), pieces=()):
    n, m = len(arrays), len(arrays) + len(after)
    free = pl.BlockSpec(memory_space=pl.ANY)

    def kernel(*refs):
        outs, sems = refs[m + n : -1], refs[-1]
        copies = [
            pltpu.make_async_copy(refs[which].at[pl.ds(at, 1)], out, sems.at[i])
            for i, ((which, at), out) in enumerate(zip(pieces, outs))
        ]
        for copy in copies:
            copy.start()
        for copy in copies:
            copy.wait()

    return pl.pallas_call(
        kernel,
        in_specs=[free] * m,
        out_specs=(free,) * n + (pl.BlockSpec(memory_space=pltpu.VMEM),) * len(pieces),
        out_shape=tuple(shape(*a.shape) for a in arrays)
        + tuple(shape(1, *arrays[which].shape[1:]) for which, _ in pieces),
        scratch_shapes=[pltpu.SemaphoreType.DMA((max(len(pieces), 1),))],
        input_output_aliases={i: i for i in range(n)},
        compiler_params=PARAMS,
        cost_estimate=cost(1, 1),
    )(*arrays, *after)


def shift(x, axis, by):
    n = lax.axis_size(axis)
    return lax.ppermute(x, axis, [(i, (i + by) % n) for i in range(n)])


def per_device(tokens, weights, cotangent):
    _, rows, width = tokens.shape
    w_rows, _, cols = weights.shape
    heads = cols // HS
    n_x, n_y = (lax.axis_size(a) for a in ("x", "y"))
    ids = jnp.stack([lax.axis_index(a) for a in ("core", "x", "zh", "y", "zl")])
    tokens = tokens.reshape(rows, width)
    half = width // lax.axis_size("zh") // 2

    swap = lambda a: shift(a, "core", 1)
    own = weights.transpose(1, 0, 2)
    left, right, other = shift(own, "y", 1), shift(own, "y", -1), shift(own, "zl", 1)
    root, mine, mine_t, given = unit_rows(ids, tokens, w_rows, True)
    _, theirs, theirs_t = unit_rows(ids, swap(tokens), w_rows, False)
    left, right, other = gate((left, right, other), (theirs,))

    left_0, right_0 = shift(mine_t, "x", 1), shift(mine_t, "x", -1)
    left_1, right_1 = shift(theirs_t, "x", 1), shift(theirs_t, "x", -1)

    near = ((0, 0), (3, 0), (1, 0), (0, 1))
    *sums, stack_0 = project(ids, mine, theirs, (own, left, right, other), near, after=(left_0, right_0))
    far, other_left, other_right, *pieces = gate(
        (shift(left, "y", 1), shift(left, "zl", 1), shift(other, "y", -1)),
        sums,
        ((0, 0), (1, 1), (2, 2)),
    )
    then = ((2, 0), (3, 1), (1, 1))
    keep, give, stack_1 = project(
        ids, mine, theirs, (far, other_left, other_right), then, sums, BF
    )
    *pieces, give = gate(
        (shift(pieces[0], "zl", 1), shift(pieces[1], "y", 1), shift(pieces[2], "y", -1), give)
    )
    pieces = (*pieces, *(swap(p) for p in pieces))
    proj, stack_0, stack_1 = project_last(
        ids, mine, given, keep, swap(give), cotangent.reshape(rows, cols), pieces, (2, 1), heads,
        (stack_0, stack_1), (left_1, right_1),
    )

    far_0, far_1 = shift(left_0, "x", 1), shift(right_1, "x", -1)
    blocks = (mine_t, theirs_t, left_0, left_1, right_0, right_1, far_0, far_1)
    spots = tuple((i, 0, by, i % 2) for i, by in enumerate((0, 0, 3, 3, 1, 1, 2, 2)))
    qkv = lax.all_to_all(proj, "x", 0, 0, tiled=True).reshape(n_x * rows, 4 * HS)
    att, head_grads = attention(qkv, (far_0, far_1))

    shards = (*pieces, stack_0, swap(stack_0), stack_1, swap(stack_1))
    places = {(2, 1): [[(3 * core + j, (0,)) for j in range(3)] for core in range(2)]}
    for first, keys in ((6, near), (8, then)):
        for i, key in enumerate(keys):
            places[key] = [[(first + core, (i, j)) for j in range(3)] for core in range(2)]
    places = [places[(by, z)] for by in range(n_y) for z in range(2)]

    head_grads = head_grads.reshape(n_x, rows, 3 * HS)
    grads = lax.all_to_all(head_grads, "x", 0, 0, tiled=True)
    part = outer(ids, blocks, spots, head_grads, swap(head_grads), (shards[7], shards[9]))

    up, down, stat = norm_halves(
        ids, grads, proj, shards, places,
        ((2, 0), (1, 1), (2, 1), (3, 0)),
        ((0, 0), (0, half), (1, 0), (1, half)),
        (2 * half + 16, 2 * half),
        width,
    )
    up, down = shift(up, "zh", 1), shift(down, "zh", -1)
    up_part, down_part, own0, own1, _ = norm_halves(
        ids, grads, proj, shards, places,
        ((1, 0), (3, 1), (0, 0), (0, 1)),
        ((0, 0), (1, 0), (2, 0), (3, 0)),
        (half,) * 4,
        width,
        (stat,),
    )
    part = lax.all_to_all(part, "y", 0, 0, tiled=True).reshape(n_y, 2, w_rows, 3 * HS)
    keep, give = split(ids, part, (own0,))
    came = shift(give, "zl", 1)
    up_2, down_2 = add_messages(up_part, up, down_part, down, stat, (came,))
    last = merge(keep, came, att.reshape(n_x, rows, HS))
    up_2, down_2 = shift(up_2, "zh", 1), shift(down_2, "zh", -1)
    last = lax.all_to_all(last, "x", 0, 0, tiled=True)
    token_grad = finish(ids, (own0, own1, up_2, up, down, down_2), tokens, root, stat)
    weight_grad, attended = unpack(last)
    return attended[None], token_grad[None], weight_grad.transpose(1, 0, 2)


def solution(mesh):
    fine = Mesh(mesh.devices.reshape(4, 2, 2, 4, 4), ("y", "zl", "core", "x", "zh"))
    dp = ("y", "zl", "core")
    return jax.shard_map(
        per_device,
        mesh=fine,
        in_specs=(P(dp, "x", None), P(dp, None, "zh"), P(dp, "x", "zh")),
        out_specs=(P(dp, "x", "zh"), P(dp, "x", "zh"), P(dp, None, "zh")),
        check_vma=False,
    )
```

profile of v0, /device:TPU:8, one launch (start us, length us, event | category | flops | bytes accessed | tf_op | source)
XLA Modules:
  0.0 198.2 jit_solution(10680496314245885125)
XLA Ops:
  0.7 1.7 collective-permute-start.7
  2.4 0.7 collective-permute-start.8
  3.1 1.7 collective-permute-start.9
  4.8 0.7 stack.23.at_ref
  5.4 4.2 %shard_map.58 = (f32[256,1]{1,0:T(8,128)}, bf16[256,2048]{1,0:T(8,128)(2,1)}, bf16[1,2048,256]{2,1,0:T(8,128)(2,1)}, bf16[256,2048]{1,0:T(8,128)(2,1)}) custom-call(s32[5]{0:T(128)} %stack.23.at_ref, bf16[256,4096]{1,0:T(8,128)(2,1)} %bitcast.28), custom_call_target="tpu_custom_call" | custom-call | flops 20000000000 | bytes 1 | tf_op jit(solution)/shard_map/pallas_call | solution.py:54
  9.6 1.5 collective-permute-start.1
  11.1 1.7 collective-permute-start.3
  12.8 3.8 %shard_map.59 = (f32[256,1]{1,0:T(8,128)}, bf16[256,2048]{1,0:T(8,128)(2,1)}, bf16[1,2048,256]{2,1,0:T(8,128)(2,1)}) custom-call(s32[5]{0:T(128)} %stack.23.at_ref, bf16[256,4096]{1,0:T(8,128)(2,1)} %collective-permute-done.tok_ref), custom_call_target="tpu_custom_call" | custom-call | flops 20000000000 | bytes 1 | tf_op jit(solution)/shard_map/pallas_call | solution.py:54
  16.7 4.7 %collective-permute-done.7.refs_0_ = bf16[3,256,512]{2,1,0:T(8,128)(2,1)S(1)} collective-permute-done((bf16[3,256,512]{2,1,0:T(8,128)(2,1)}, bf16[3,256,512]{2,1,0:T(8,128)(2,1)S(1)}, u32[]{:S(2)}, u32[]{:S(2)}) %collective-permute-start.7) | collective-permute-done | bytes 786464 | tf_op jit(solution)/shard_map/ppermute | solution.py:508
  21.3 0.9 collective-permute-done.8.refs_1_
  22.2 0.6 collective-permute-done.9.refs_2_
  23.1 0.6 copy-done.11
  23.7 1.4 collective-permute-start.10
  25.1 1.7 collective-permute-start.11
  26.8 0.6 collective-permute-start.12
  27.4 8.4 %collective-permute-done.1.refs_4_.refs_2_ = bf16[1,2048,256]{2,1,0:T(8,128)(2,1)} collective-permute-done((bf16[1,2048,256]{2,1,0:T(8,128)(2,1)}, bf16[1,2048,256]{2,1,0:T(8,128)(2,1)}, u32[]{:S(2)}, u32[]{:S(2)}) %collective-permute-start.1) | collective-permute-done | bytes 1048608 | tf_op jit(solution)/shard_map/ppermute | solution.py:508
  35.8 1.5 collective-permute-start.4
  37.3 0.5 collective-permute-start.2
  37.8 0.5 copy-done.5
  38.3 6.3 %shard_map.61 = (f32[256,1536]{1,0:T(8,128)}, f32[256,1536]{1,0:T(8,128)}, bf16[4,3,256,512]{3,2,1,0:T(8,128)(2,1)}) custom-call(s32[5]{0:T(128)} %stack.23.at_ref, bf16[256,2048]{1,0:T(8,128)(2,1)} %get-tuple-element.48.mine_ref, bf16[256,2048]{1,0:T(8,128)(2,1)} %get-tuple-element.50.refs_3_.theirs_ref, bf16[3,256,512]{2,1,0:T(8,128)(2,1)} %bitcast.24, ...), custom_call_target="tpu_custom_call" | custom-call | flops 1 | bytes 1 | tf_op jit(solution)/shard_map/pallas_call | solution.py:103
  44.7 0.6 collective-permute-done.12.refs_2_
  45.8 2.0 %shard_map.62 = (bf16[3,256,512]{2,1,0:T(8,128)(2,1)}, bf16[3,256,512]{2,1,0:T(8,128)(2,1)}, bf16[3,256,512]{2,1,0:T(8,128)(2,1)}, bf16[1,256,512]{2,1,0:T(8,128...) custom-call(bf16[3,256,512]{2,1,0:T(8,128)(2,1)} %copy-done.7, ...), custom_call_target="tpu_custom_call", output_to_operand_aliasing={{0}: (0, {}), {1}: (1, {}), {2}: (2, {})} | custom-call | flops 1 | bytes 1 | tf_op jit(solution)/shard_map/pallas_call | solution.py:493
  47.8 1.1 collective-permute-start.13
  48.9 1.7 collective-permute-start.14
  50.9 6.2 %shard_map.63 = (f32[256,1536]{1,0:T(8,128)}, bf16[256,1536]{1,0:T(8,128)(2,1)}, bf16[3,3,256,512]{3,2,1,0:T(8,128)(2,1)}) custom-call(s32[5]{0:T(128)} %stack.23.at_ref, bf16[256,2048]{1,0:T(8,128)(2,1)} %get-tuple-element.48.mine_ref, bf16[256,2048]{1,0:T(8,128)(2,1)} %get-tuple-element.50.refs_3_.theirs_ref, ...), custom_call_target="tpu_custom_call" | custom-call | flops 1 | bytes 1 | tf_op jit(solution)/shard_map/pallas_call | solution.py:103
  57.2 0.4 collective-permute-done.15.refs_2_
  58.4 0.5 collective-permute-start.17
  59.0 0.8 collective-permute-done.4.refs_9_.refs_5_
  59.8 2.4 %collective-permute-done.2.refs_8_.refs_3_ = bf16[1,2048,256]{2,1,0:T(8,128)(2,1)S(1)} collective-permute-done((bf16[1,2048,256]{2,1,0:T(8,128)(2,1)}, bf16[1,2048,256]{2,1,0:T(8,128)(2,1)S(1)}, u32[]{:S(2)}, u32[]{:S(2)}) %collective-permute-start.2) | collective-permute-done | bytes 1048608 | tf_op jit(solution)/shard_map/ppermute | solution.py:508
  62.2 3.2 %collective-permute-start.6 = (bf16[1,2048,256]{2,1,0:T(8,128)(2,1)}, bf16[1,2048,256]{2,1,0:T(8,128)(2,1)}, u32[]{:S(2)}, u32[]{:S(2)}) collective-permute-start(bf16[1,2048,256]{2,1,0:T(8,128)(2,1)} %collective-permute-done.4.refs_9_.refs_5_), channel_id=1, source_target_pairs={{0,12},{4,0},{8,4},{12,8},{1,13},{5,1},{9,5},{13,9},{2,14},{6,2},{... | collective-permute-start | bytes 3145736 | tf_op jit(solution)/shard_map/ppermute | solution.py:508
  65.5 0.6 copy-done.13
  66.5 4.4 %shard_map.65 = (bf16[4,256,512]{2,1,0:T(8,128)(2,1)}, bf16[4,3,256,512]{3,2,1,0:T(8,128)(2,1)}, bf16[3,3,256,512]{3,2,1,0:T(8,128)(2,1)}) custom-call(s32[5]{0:T(128)} %stack.23.at_ref, bf16[256,2048]{1,0:T(8,128)(2,1)} %get-tuple-element.48.mine_ref, ...), custom_call_target="tpu_custom_call", output_to_operand_aliasing={{1}: (12, {}), {2}: (13, {})} | custom-call | flops 1 | bytes 1 | tf_op jit(solution)/shard_map/pallas_call | solution.py:141
  70.9 4.2 %all-to-all-start = ((bf16[4,256,512]{2,1,0:T(8,128)(2,1)}), bf16[4,256,512]{2,1,0:T(8,128)(2,1)}, u32[]{:S(2)}, u32[]{:S(2)}) async-start(bf16[4,256,512]{2,1,0:T(8,128)(2,1)} %get-tuple-element.70.p_ref), calls=%async_computation | async-start | bytes 2097152 | tf_op jit(solution)/shard_map/all_to_all | solution.py:553
  75.3 0.5 collective-permute-start.22
  75.8 14.0 %collective-permute-done.5.refs_0_.refs_6_ = bf16[1,2048,256]{2,1,0:T(8,128)(2,1)} collective-permute-done((bf16[1,2048,256]{2,1,0:T(8,128)(2,1)}, bf16[1,2048,256]{2,1,0:T(8,128)(2,1)}, u32[]{:S(2)}, u32[]{:S(2)}) %collective-permute-start.5) | collective-permute-done | bytes 1048608 | tf_op jit(solution)/shard_map/ppermute | solution.py:508
  89.8 9.4 %all-to-all-done = bf16[4,256,512]{2,1,0:T(8,128)(2,1)} async-done(((bf16[4,256,512]{2,1,0:T(8,128)(2,1)}), bf16[4,256,512]{2,1,0:T(8,128)(2,1)}, u32[]{:S(2)}, u32[]{:S(2)}) %all-to-all-start) | async-done | bytes 1048608 | tf_op jit(solution)/shard_map/all_to_all | solution.py:553
  99.2 6.2 %shard_map.66 = (bf16[1024,128]{1,0:T(8,128)(2,1)}, bf16[1024,384]{1,0:T(8,128)(2,1)}) custom-call(bf16[1024,512]{1,0:T(8,128)(2,1)} %bitcast.8.qkv_ref, bf16[1,2048,256]{2,1,0:T(8,128)(2,1)} %collective-permute-done.5.refs_0_.refs_6_, bf16[1,2048,256]{2,1,0:T(8,128)(2,1)} %collective-permute-done.6.refs_1_.refs_7_), custom_call_target="tpu_custom_call" | custom-call | flops 20000000000 | bytes 1 | tf_op jit(solution)/shard_map/pallas_call | solution.py:192
  105.4 4.4 %all-to-all-start.2 = ((bf16[4,256,384]{2,1,0:T(8,128)(2,1)}), bf16[4,256,384]{2,1,0:T(8,128)(2,1)}, u32[]{:S(2)}, u32[]{:S(2)}) async-start(bf16[4,256,384]{2,1,0:T(8,128)(2,1)} %bitcast.19), calls=%async_computation.2 | async-start | bytes 1572864 | tf_op jit(solution)/shard_map/all_to_all | solution.py:564
  109.8 1.7 copy-done
  111.5 9.3 %shard_map.67 = bf16[2048,384]{1,0:T(8,128)(2,1)} custom-call(s32[5]{0:T(128)} %stack.23.at_ref, bf16[1,2048,256]{2,1,0:T(8,128)(2,1)} %get-tuple-element.46.refs_0_, bf16[1,2048,256]{2,1,0:T(8,128)(2,1)} %get-tuple-element.47.refs_1_, bf16[1,2048,256]{2,1,0:T(8,128)(2,1)} %collective-permute-done.1.refs_4_.refs_2_, bf16[1,2048,256]{2,1,0:T(8,128)(2,1)} %copy-done.6, ...), custom_call_target="tpu_custom_call" | custom-call | flops 1 | bytes 1 | tf_op jit(solution)/shard_map/pallas_call | solution.py:391
  120.8 2.0 %all-to-all-done.2.g_ref = bf16[4,256,384]{2,1,0:T(8,128)(2,1)} async-done(((bf16[4,256,384]{2,1,0:T(8,128)(2,1)}), bf16[4,256,384]{2,1,0:T(8,128)(2,1)}, u32[]{:S(2)}, u32[]{:S(2)}) %all-to-all-start.2) | async-done | bytes 786464 | tf_op jit(solution)/shard_map/all_to_all | solution.py:564
  122.9 5.7 %all-to-all-start.1 = ((bf16[4,512,384]{2,1,0:T(8,128)(2,1)}), bf16[4,512,384]{2,1,0:T(8,128)(2,1)S(1)}, u32[]{:S(2)}, u32[]{:S(2)}) async-start(bf16[4,512,384]{2,1,0:T(8,128)(2,1)} %bitcast.16), calls=%async_computation.1 | async-start | bytes 3145728 | tf_op jit(solution)/shard_map/all_to_all | solution.py:583
  128.5 7.7 %shard_map.68 = (bf16[1040,256]{1,0:T(8,128)(2,1)}, bf16[1024,256]{1,0:T(8,128)(2,1)}, f32[1,256]{1,0:T(1,128)}) custom-call(s32[5]{0:T(128)} %stack.23.at_ref, bf16[4,256,384]{2,1,0:T(8,128)(2,1)} %all-to-all-done.2.g_ref, bf16[4,256,512]{2,1,0:T(8,128)(2,1)} %get-tuple-element.70.p_ref, bf16[1,256,512]{2,1,0:T(8,128)(2,1)} %get-tuple-element.65.refs_0_, ...), custom_call_target="tpu_custom_call" | custom-call | flops 1 | bytes 1 | tf_op jit(solution)/shard_map/pallas_call | solution.py:277
  136.3 3.4 %collective-permute-start.24 = (bf16[1040,256]{1,0:T(8,128)(2,1)}, bf16[1040,256]{1,0:T(8,128)(2,1)S(1)}, u32[]{:S(2)}, u32[]{:S(2)}) collective-permute-start(bf16[1040,256]{1,0:T(8,128)(2,1)} %get-tuple-element.82), channel_id=1, source_target_pairs={{0,1},{1,2},{2,3},{3,0},{4,5},{5,6},{6,7},{7,4},{8,9},{9,10},{10,1... | collective-permute-start | bytes 1597448 | tf_op jit(solution)/shard_map/ppermute | solution.py:508
  139.6 2.2 %collective-permute-start.25 = (bf16[1024,256]{1,0:T(8,128)(2,1)}, bf16[1024,256]{1,0:T(8,128)(2,1)S(1)}, u32[]{:S(2)}, u32[]{:S(2)}) collective-permute-start(bf16[1024,256]{1,0:T(8,128)(2,1)} %get-tuple-element.84), channel_id=1, source_target_pairs={{0,3},{1,0},{2,1},{3,2},{4,7},{5,4},{6,5},{7,6},{8,11},{9,8},{10,9... | collective-permute-start | bytes 1572872 | tf_op jit(solution)/shard_map/ppermute | solution.py:508
  141.8 7.6 %shard_map.69 = (bf16[512,256]{1,0:T(8,128)(2,1)}, bf16[512,256]{1,0:T(8,128)(2,1)}, bf16[512,256]{1,0:T(8,128)(2,1)}, bf16[512,256]{1,0:T(8,128)(2,1)}, f32[1,256]{1,0:T(1,128)}) custom-call(s32[5]{0:T(128)} %stack.23.at_ref, bf16[4,256,384]{2,1,0:T(8,128)(2,1)} %all-to-all-done.2.g_ref, bf16[4,256,512]{2,1,0:T(8,128)(2,1)} %get-tuple-element.70.p_ref, ...), custom_call_target="tpu_custom_call" | custom-call | flops 1 | bytes 1 | tf_op jit(solution)/shard_map/pallas_call | solution.py:277
  149.5 1.1 copy-done.1
  150.6 2.3 %shard_map.70 = (f32[256,384]{1,0:T(8,128)}, bf16[256,384]{1,0:T(8,128)(2,1)}) custom-call(s32[5]{0:T(128)} %stack.23.at_ref, bf16[4,2,256,384]{3,2,1,0:T(8,128)(2,1)} %bitcast.17, bf16[512,256]{1,0:T(8,128)(2,1)} %get-tuple-element.75.refs_0_.own0), custom_call_target="tpu_custom_call" | custom-call | flops 1 | bytes 1 | tf_op jit(solution)/shard_map/pallas_call | solution.py:419
  152.9 1.0 collective-permute-start.23
  153.9 11.6 %collective-permute-done.25.down_in.down0 = bf16[1024,256]{1,0:T(8,128)(2,1)S(1)} collective-permute-done((bf16[1024,256]{1,0:T(8,128)(2,1)}, bf16[1024,256]{1,0:T(8,128)(2,1)S(1)}, u32[]{:S(2)}, u32[]{:S(2)}) %collective-permute-start.25) | collective-permute-done | bytes 524320 | tf_op jit(solution)/shard_map/ppermute | solution.py:508
  165.5 0.6 collective-permute-done.24.up_in.stat_in.up1
  166.1 3.1 %collective-permute-done.23.came_ref.refs_0_ = bf16[256,384]{1,0:T(8,128)(2,1)S(1)} collective-permute-done((bf16[256,384]{1,0:T(8,128)(2,1)}, bf16[256,384]{1,0:T(8,128)(2,1)S(1)}, u32[]{:S(2)}, u32[]{:S(2)}) %collective-permute-start.23) | collective-permute-done | bytes 196640 | tf_op jit(solution)/shard_map/ppermute | solution.py:508
  169.3 0.7 copy-done.16
  169.9 2.2 %shard_map.73 = (bf16[528,256]{1,0:T(8,128)(2,1)}, bf16[528,256]{1,0:T(8,128)(2,1)}) custom-call(bf16[512,256]{1,0:T(8,128)(2,1)} %get-tuple-element.81.up_part, bf16[1040,256]{1,0:T(8,128)(2,1)} %copy-done.15, bf16[1040,256]{1,0:T(8,128)(2,1)} %copy-done.15, bf16[512,256]{1,0:T(8,128)(2,1)} %get-tuple-element.83.down_part, bf16[1024,256]{1,0:T(8,128)(2,1)} %copy-done.18, ...), custom_call_target="tpu_custom_call" | custom-call | flops 1 | bytes 1 | tf_op jit(solution)/shard_map/pallas_call | solution.py:307
  172.2 1.5 collective-permute-start.26
  173.7 2.7 %collective-permute-start.27 = (bf16[528,256]{1,0:T(8,128)(2,1)}, bf16[528,256]{1,0:T(8,128)(2,1)S(1)}, u32[]{:S(2)}, u32[]{:S(2)}) collective-permute-start(bf16[528,256]{1,0:T(8,128)(2,1)} %get-tuple-element.86), channel_id=1, source_target_pairs={{0,3},{1,0},{2,1},{3,2},{4,7},{5,4},{6,5},{7,6},{8,11},{9,8},{10,9... | collective-permute-start | bytes 811016 | tf_op jit(solution)/shard_map/ppermute | solution.py:508
  176.3 2.2 %shard_map.71 = bf16[4,256,512]{2,1,0:T(8,128)(2,1)} custom-call(f32[256,384]{1,0:T(8,128)} %get-tuple-element.76.keep_ref, bf16[256,384]{1,0:T(8,128)(2,1)} %copy-done.16, bf16[4,256,128]{2,1,0:T(8,128)(2,1)} %bitcast.26), custom_call_target="tpu_custom_call" | custom-call | flops 1 | bytes 1 | tf_op jit(solution)/shard_map/pallas_call | solution.py:443
  178.6 3.5 %all-to-all-start.3 = ((bf16[4,256,512]{2,1,0:T(8,128)(2,1)}), bf16[4,256,512]{2,1,0:T(8,128)(2,1)S(1)}, u32[]{:S(2)}, u32[]{:S(2)}) async-start(bf16[4,256,512]{2,1,0:T(8,128)(2,1)} %shard_map.71), calls=%async_computation.3 | async-start | bytes 2097152 | tf_op jit(solution)/shard_map/all_to_all | solution.py:589
  182.1 4.3 %collective-permute-done.26.up0 = bf16[528,256]{1,0:T(8,128)(2,1)S(1)} collective-permute-done((bf16[528,256]{1,0:T(8,128)(2,1)}, bf16[528,256]{1,0:T(8,128)(2,1)S(1)}, u32[]{:S(2)}, u32[]{:S(2)}) %collective-permute-start.26) | collective-permute-done | bytes 270368 | tf_op jit(solution)/shard_map/ppermute | solution.py:508
  186.4 1.1 collective-permute-done.27.down1
  187.5 0.7 copy-done.20
  188.2 3.5 %shard_map.74 = bf16[256,1024]{1,0:T(8,128)(2,1)} custom-call(s32[5]{0:T(128)} %stack.23.at_ref, bf16[512,256]{1,0:T(8,128)(2,1)} %get-tuple-element.75.refs_0_.own0, bf16[512,256]{1,0:T(8,128)(2,1)} %get-tuple-element.80.own1, bf16[528,256]{1,0:T(8,128)(2,1)} %copy-done.19, bf16[1040,256]{1,0:T(8,128)(2,1)} %copy-done.15, bf16[1024,256]{1,0:T(8,128)(2,1)} %copy-done.18, ...), custom_call_target="tpu_custom_call" | custom-call | flops 20000000000 | bytes 1 | tf_op jit(solution)/shard_map/pallas_call | solution.py:341
  191.7 4.7 %all-to-all-done.3.in_ref = bf16[4,256,512]{2,1,0:T(8,128)(2,1)S(1)} async-done(((bf16[4,256,512]{2,1,0:T(8,128)(2,1)}), bf16[4,256,512]{2,1,0:T(8,128)(2,1)S(1)}, u32[]{:S(2)}, u32[]{:S(2)}) %all-to-all-start.3) | async-done | bytes 1048608 | tf_op jit(solution)/shard_map/all_to_all | solution.py:589
  196.3 1.9 shard_map.72
  (60 shorter events, 2.7 us)
Async XLA Ops:
  0.6 10.5 %collective-permute-start = (bf16[256,4096]{1,0:T(8,128)(2,1)}, bf16[256,4096]{1,0:T(8,128)(2,1)}, u32[]{:S(2)}, u32[]{:S(2)}) collective-permute-start(bf16[256,4096]{1,0:T(8,128)(2,1)} %bitcast.27), channel_id=1, source_target_pairs={{0,16},{16,0},{1,17},{17,1},{2,18},{18,2},{3,19},{19,3},{4,20},{20... | collective-permute-start | bytes 6291464 | tf_op jit(solution)/shard_map/ppermute | solution.py:508
  0.7 20.6 %collective-permute-start.7 = (bf16[3,256,512]{2,1,0:T(8,128)(2,1)}, bf16[3,256,512]{2,1,0:T(8,128)(2,1)S(1)}, u32[]{:S(2)}, u32[]{:S(2)}) collective-permute-start(bf16[3,256,512]{2,1,0:T(8,128)(2,1)} %bitcast.21), channel_id=1, source_target_pairs={{0,64},{64,128},{128,192},{192,0},{1,65},{65,129},{129,193},{193,1... | collective-permute-start | bytes 2359304 | tf_op jit(solution)/shard_map/ppermute | solution.py:508
  2.4 19.8 %collective-permute-start.8 = (bf16[3,256,512]{2,1,0:T(8,128)(2,1)}, bf16[3,256,512]{2,1,0:T(8,128)(2,1)S(1)}, u32[]{:S(2)}, u32[]{:S(2)}) collective-permute-start(bf16[3,256,512]{2,1,0:T(8,128)(2,1)} %bitcast.22), channel_id=1, source_target_pairs={{0,192},{64,0},{128,64},{192,128},{1,193},{65,1},{129,65},{193,129... | collective-permute-start | bytes 2359304 | tf_op jit(solution)/shard_map/ppermute | solution.py:508
  3.1 19.7 %collective-permute-start.9 = (bf16[3,256,512]{2,1,0:T(8,128)(2,1)}, bf16[3,256,512]{2,1,0:T(8,128)(2,1)S(1)}, u32[]{:S(2)}, u32[]{:S(2)}) collective-permute-start(bf16[3,256,512]{2,1,0:T(8,128)(2,1)} %bitcast.23), channel_id=1, source_target_pairs={{0,32},{32,0},{1,33},{33,1},{2,34},{34,2},{3,35},{35,3},{4,36},{36... | collective-permute-start | bytes 2359304 | tf_op jit(solution)/shard_map/ppermute | solution.py:508
  9.6 26.2 %collective-permute-start.1 = (bf16[1,2048,256]{2,1,0:T(8,128)(2,1)}, bf16[1,2048,256]{2,1,0:T(8,128)(2,1)}, u32[]{:S(2)}, u32[]{:S(2)}) collective-permute-start(bf16[1,2048,256]{2,1,0:T(8,128)(2,1)} %get-tuple-element.46.refs_0_), channel_id=1, source_target_pairs={{0,4},{4,8},{8,12},{12,0},{1,5},{5,9},{9,13},{13,1},{2,6},{6,10},{... | collective-permute-start | bytes 3145736 | tf_op jit(solution)/shard_map/ppermute | solution.py:508
  11.1 26.2 %collective-permute-start.3 = (bf16[1,2048,256]{2,1,0:T(8,128)(2,1)}, bf16[1,2048,256]{2,1,0:T(8,128)(2,1)S(1)}, u32[]{:S(2)}, u32[]{:S(2)}) collective-permute-start(bf16[1,2048,256]{2,1,0:T(8,128)(2,1)} %get-tuple-element.46.refs_0_), channel_id=1, source_target_pairs={{0,12},{4,0},{8,4},{12,8},{1,13},{5,1},{9,5},{13,9},{2,14},{6,2},{... | collective-permute-start | bytes 3145736 | tf_op jit(solution)/shard_map/ppermute | solution.py:508
  21.3 1.5 copy-start.9
  22.2 0.9 copy-start.10
  22.8 0.9 copy-start.11
  23.7 20.9 %collective-permute-start.10 = (bf16[3,256,512]{2,1,0:T(8,128)(2,1)}, bf16[3,256,512]{2,1,0:T(8,128)(2,1)S(1)}, u32[]{:S(2)}, u32[]{:S(2)}) collective-permute-start(bf16[3,256,512]{2,1,0:T(8,128)(2,1)} %get-tuple-element.51.refs_1_), channel_id=1, source_target_pairs={{0,64},{64,128},{128,192},{192,0},{1,65},{65,129},{129,193},{193,1... | collective-permute-start | bytes 2359304 | tf_op jit(solution)/shard_map/ppermute | solution.py:508
  25.1 19.5 %collective-permute-start.11 = (bf16[3,256,512]{2,1,0:T(8,128)(2,1)}, bf16[3,256,512]{2,1,0:T(8,128)(2,1)S(1)}, u32[]{:S(2)}, u32[]{:S(2)}) collective-permute-start(bf16[3,256,512]{2,1,0:T(8,128)(2,1)} %get-tuple-element.51.refs_1_), channel_id=1, source_target_pairs={{0,32},{32,0},{1,33},{33,1},{2,34},{34,2},{3,35},{35,3},{4,36},{36... | collective-permute-start | bytes 2359304 | tf_op jit(solution)/shard_map/ppermute | solution.py:508
  26.8 18.4 %collective-permute-start.12 = (bf16[3,256,512]{2,1,0:T(8,128)(2,1)}, bf16[3,256,512]{2,1,0:T(8,128)(2,1)}, u32[]{:S(2)}, u32[]{:S(2)}) collective-permute-start(bf16[3,256,512]{2,1,0:T(8,128)(2,1)} %get-tuple-element.52.refs_3_), channel_id=1, source_target_pairs={{0,192},{64,0},{128,64},{192,128},{1,193},{65,1},{129,65},{193,129... | collective-permute-start | bytes 2359304 | tf_op jit(solution)/shard_map/ppermute | solution.py:508
  35.8 24.1 %collective-permute-start.4 = (bf16[1,2048,256]{2,1,0:T(8,128)(2,1)}, bf16[1,2048,256]{2,1,0:T(8,128)(2,1)}, u32[]{:S(2)}, u32[]{:S(2)}) collective-permute-start(bf16[1,2048,256]{2,1,0:T(8,128)(2,1)} %get-tuple-element.47.refs_1_), channel_id=1, source_target_pairs={{0,12},{4,0},{8,4},{12,8},{1,13},{5,1},{9,5},{13,9},{2,14},{6,2},{... | collective-permute-start | bytes 3145736 | tf_op jit(solution)/shard_map/ppermute | solution.py:508
  37.3 1.0 copy-start.5
  37.3 24.9 %collective-permute-start.2 = (bf16[1,2048,256]{2,1,0:T(8,128)(2,1)}, bf16[1,2048,256]{2,1,0:T(8,128)(2,1)S(1)}, u32[]{:S(2)}, u32[]{:S(2)}) collective-permute-start(bf16[1,2048,256]{2,1,0:T(8,128)(2,1)} %get-tuple-element.47.refs_1_), channel_id=1, source_target_pairs={{0,4},{4,8},{8,12},{12,0},{1,5},{5,9},{9,13},{13,1},{2,6},{6,10},{... | collective-permute-start | bytes 3145736 | tf_op jit(solution)/shard_map/ppermute | solution.py:508
  44.6 0.9 copy-start.7
  44.7 1.1 copy-start.8
  47.8 9.4 %collective-permute-start.13 = (bf16[1,256,512]{2,1,0:T(8,128)(2,1)}, bf16[1,256,512]{2,1,0:T(8,128)(2,1)S(1)}, u32[]{:S(2)}, u32[]{:S(2)}) collective-permute-start(bf16[1,256,512]{2,1,0:T(8,128)(2,1)} %get-tuple-element.60), channel_id=1, source_target_pairs={{0,32},{32,0},{1,33},{33,1},{2,34},{34,2},{3,35},{35,3},{4,36},{36... | collective-permute-start | bytes 786440 | tf_op jit(solution)/shard_map/ppermute | solution.py:508
  48.9 8.3 %collective-permute-start.14 = (bf16[1,256,512]{2,1,0:T(8,128)(2,1)}, bf16[1,256,512]{2,1,0:T(8,128)(2,1)S(1)}, u32[]{:S(2)}, u32[]{:S(2)}) collective-permute-start(bf16[1,256,512]{2,1,0:T(8,128)(2,1)} %get-tuple-element.61), channel_id=1, source_target_pairs={{0,64},{64,128},{128,192},{192,0},{1,65},{65,129},{129,193},{193,1... | collective-permute-start | bytes 786440 | tf_op jit(solution)/shard_map/ppermute | solution.py:508
  50.6 6.9 %collective-permute-start.15 = (bf16[1,256,512]{2,1,0:T(8,128)(2,1)}, bf16[1,256,512]{2,1,0:T(8,128)(2,1)S(1)}, u32[]{:S(2)}, u32[]{:S(2)}) collective-permute-start(bf16[1,256,512]{2,1,0:T(8,128)(2,1)} %get-tuple-element.62), channel_id=1, source_target_pairs={{0,192},{64,0},{128,64},{192,128},{1,193},{65,1},{129,65},{193,129... | collective-permute-start | bytes 786440 | tf_op jit(solution)/shard_map/ppermute | solution.py:508
  57.2 0.7 copy-start.2
  57.2 0.8 copy-start.3
  57.6 0.7 copy-start.4
  58.3 7.2 %collective-permute-start.16 = (bf16[256,1536]{1,0:T(8,128)(2,1)}, bf16[256,1536]{1,0:T(8,128)(2,1)S(1)}, u32[]{:S(2)}, u32[]{:S(2)}) collective-permute-start(bf16[256,1536]{1,0:T(8,128)(2,1)} %get-tuple-element.64), channel_id=1, source_target_pairs={{0,16},{16,0},{1,17},{17,1},{2,18},{18,2},{3,19},{19,3},{4,20},{20... | collective-permute-start | bytes 2359304 | tf_op jit(solution)/shard_map/ppermute | solution.py:508
  58.4 3.8 %collective-permute-start.17 = (bf16[1,256,512]{2,1,0:T(8,128)(2,1)}, bf16[1,256,512]{2,1,0:T(8,128)(2,1)S(1)}, u32[]{:S(2)}, u32[]{:S(2)}) collective-permute-start(bf16[1,256,512]{2,1,0:T(8,128)(2,1)} %get-tuple-element.65.refs_0_), channel_id=1, source_target_pairs={{0,16},{16,0},{1,17},{17,1},{2,18},{18,2},{3,19},{19,3},{4,20},{20... | collective-permute-start | bytes 786440 | tf_op jit(solution)/shard_map/ppermute | solution.py:508
  58.9 6.6 %collective-permute-start.18 = (bf16[1,256,512]{2,1,0:T(8,128)(2,1)}, bf16[1,256,512]{2,1,0:T(8,128)(2,1)S(1)}, u32[]{:S(2)}, u32[]{:S(2)}) collective-permute-start(bf16[1,256,512]{2,1,0:T(8,128)(2,1)} %get-tuple-element.66.refs_1_), channel_id=1, source_target_pairs={{0,16},{16,0},{1,17},{17,1},{2,18},{18,2},{3,19},{19,3},{4,20},{20... | collective-permute-start | bytes 786440 | tf_op jit(solution)/shard_map/ppermute | solution.py:508
  59.8 5.6 %collective-permute-start.19 = (bf16[1,256,512]{2,1,0:T(8,128)(2,1)}, bf16[1,256,512]{2,1,0:T(8,128)(2,1)S(1)}, u32[]{:S(2)}, u32[]{:S(2)}) collective-permute-start(bf16[1,256,512]{2,1,0:T(8,128)(2,1)} %get-tuple-element.67.refs_2_), channel_id=1, source_target_pairs={{0,16},{16,0},{1,17},{17,1},{2,18},{18,2},{3,19},{19,3},{4,20},{20... | collective-permute-start | bytes 786440 | tf_op jit(solution)/shard_map/ppermute | solution.py:508
  62.2 3.3 %copy-start.6 = (bf16[1,2048,256]{2,1,0:T(8,128)(2,1)}, bf16[1,2048,256]{2,1,0:T(8,128)(2,1)S(1)}, u32[]{:S(2)}) copy-start(bf16[1,2048,256]{2,1,0:T(8,128)(2,1)S(1)} %collective-permute-done.2.refs_8_.refs_3_) | copy-start | bytes 3145732
  62.2 27.5 %collective-permute-start.5 = (bf16[1,2048,256]{2,1,0:T(8,128)(2,1)}, bf16[1,2048,256]{2,1,0:T(8,128)(2,1)}, u32[]{:S(2)}, u32[]{:S(2)}) collective-permute-start(bf16[1,2048,256]{2,1,0:T(8,128)(2,1)} %collective-permute-done.1.refs_4_.refs_2_), channel_id=1, source_target_pairs={{0,4},{4,8},{8,12},{12,0},{1,5},{5,9},{9,13},{13,1},{2,6},{6,10},{... | collective-permute-start | bytes 3145736 | tf_op jit(solution)/shard_map/ppermute | solution.py:508
  62.2 3.3 %copy-start.12 = (bf16[1,256,512]{2,1,0:T(8,128)(2,1)}, bf16[1,256,512]{2,1,0:T(8,128)(2,1)S(1)}, u32[]{:S(2)}) copy-start(bf16[1,256,512]{2,1,0:T(8,128)(2,1)S(1)} %collective-permute-done.17.refs_3_) | copy-start | bytes 786436
  62.2 27.5 %collective-permute-start.6 = (bf16[1,2048,256]{2,1,0:T(8,128)(2,1)}, bf16[1,2048,256]{2,1,0:T(8,128)(2,1)}, u32[]{:S(2)}, u32[]{:S(2)}) collective-permute-start(bf16[1,2048,256]{2,1,0:T(8,128)(2,1)} %collective-permute-done.4.refs_9_.refs_5_), channel_id=1, source_target_pairs={{0,12},{4,0},{8,4},{12,8},{1,13},{5,1},{9,5},{13,9},{2,14},{6,2},{... | collective-permute-start | bytes 3145736 | tf_op jit(solution)/shard_map/ppermute | solution.py:508
  65.5 0.7 copy-start.13
  65.5 0.8 copy-start.14
  65.5 1.0 copy-start.17
  70.9 28.3 %all-to-all-start = ((bf16[4,256,512]{2,1,0:T(8,128)(2,1)}), bf16[4,256,512]{2,1,0:T(8,128)(2,1)}, u32[]{:S(2)}, u32[]{:S(2)}) async-start(bf16[4,256,512]{2,1,0:T(8,128)(2,1)} %get-tuple-element.70.p_ref), calls=%async_computation | async-start | bytes 2097152 | tf_op jit(solution)/shard_map/all_to_all | solution.py:553
  75.2 34.6 %collective-permute-start.21 = (bf16[4,3,256,512]{3,2,1,0:T(8,128)(2,1)}, bf16[4,3,256,512]{3,2,1,0:T(8,128)(2,1)S(1)}, u32[]{:S(2)}, u32[]{:S(2)}) collective-permute-start(bf16[4,3,256,512]{3,2,1,0:T(8,128)(2,1)} %get-tuple-element.72.refs_6_), channel_id=1, source_target_pairs={{0,16},{16,0},{1,17},{17,1},{2,18},{18,2},{3,19},{19,3},{4,20},{20... | collective-permute-start | bytes 9437192 | tf_op jit(solution)/shard_map/ppermute | solution.py:508
  75.3 34.5 %collective-permute-start.22 = (bf16[3,3,256,512]{3,2,1,0:T(8,128)(2,1)}, bf16[3,3,256,512]{3,2,1,0:T(8,128)(2,1)}, u32[]{:S(2)}, u32[]{:S(2)}) collective-permute-start(bf16[3,3,256,512]{3,2,1,0:T(8,128)(2,1)} %get-tuple-element.73.refs_8_), channel_id=1, source_target_pairs={{0,16},{16,0},{1,17},{17,1},{2,18},{18,2},{3,19},{19,3},{4,20},{20... | collective-permute-start | bytes 7077896 | tf_op jit(solution)/shard_map/ppermute | solution.py:508
  105.4 4.4 %collective-permute-start.20 = (bf16[4,256,384]{2,1,0:T(8,128)(2,1)}, bf16[4,256,384]{2,1,0:T(8,128)(2,1)}, u32[]{:S(2)}, u32[]{:S(2)}) collective-permute-start(bf16[4,256,384]{2,1,0:T(8,128)(2,1)} %bitcast.18), channel_id=1, source_target_pairs={{0,16},{16,0},{1,17},{17,1},{2,18},{18,2},{3,19},{19,3},{4,20},{20... | collective-permute-start | bytes 2359304 | tf_op jit(solution)/shard_map/ppermute | solution.py:508
  105.4 17.5 %all-to-all-start.2 = ((bf16[4,256,384]{2,1,0:T(8,128)(2,1)}), bf16[4,256,384]{2,1,0:T(8,128)(2,1)}, u32[]{:S(2)}, u32[]{:S(2)}) async-start(bf16[4,256,384]{2,1,0:T(8,128)(2,1)} %bitcast.19), calls=%async_computation.2 | async-start | bytes 1572864 | tf_op jit(solution)/shard_map/all_to_all | solution.py:564
  109.8 1.7 copy-start
  122.9 26.6 %all-to-all-start.1 = ((bf16[4,512,384]{2,1,0:T(8,128)(2,1)}), bf16[4,512,384]{2,1,0:T(8,128)(2,1)S(1)}, u32[]{:S(2)}, u32[]{:S(2)}) async-start(bf16[4,512,384]{2,1,0:T(8,128)(2,1)} %bitcast.16), calls=%async_computation.1 | async-start | bytes 3145728 | tf_op jit(solution)/shard_map/all_to_all | solution.py:583
  136.3 29.9 %collective-permute-start.24 = (bf16[1040,256]{1,0:T(8,128)(2,1)}, bf16[1040,256]{1,0:T(8,128)(2,1)S(1)}, u32[]{:S(2)}, u32[]{:S(2)}) collective-permute-start(bf16[1040,256]{1,0:T(8,128)(2,1)} %get-tuple-element.82), channel_id=1, source_target_pairs={{0,1},{1,2},{2,3},{3,0},{4,5},{5,6},{6,7},{7,4},{8,9},{9,10},{10,1... | collective-permute-start | bytes 1597448 | tf_op jit(solution)/shard_map/ppermute | solution.py:508
  139.6 25.9 %collective-permute-start.25 = (bf16[1024,256]{1,0:T(8,128)(2,1)}, bf16[1024,256]{1,0:T(8,128)(2,1)S(1)}, u32[]{:S(2)}, u32[]{:S(2)}) collective-permute-start(bf16[1024,256]{1,0:T(8,128)(2,1)} %get-tuple-element.84), channel_id=1, source_target_pairs={{0,3},{1,0},{2,1},{3,2},{4,7},{5,4},{6,5},{7,6},{8,11},{9,8},{10,9... | collective-permute-start | bytes 1572872 | tf_op jit(solution)/shard_map/ppermute | solution.py:508
  149.4 1.1 copy-start.1
  152.9 16.4 %collective-permute-start.23 = (bf16[256,384]{1,0:T(8,128)(2,1)}, bf16[256,384]{1,0:T(8,128)(2,1)S(1)}, u32[]{:S(2)}, u32[]{:S(2)}) collective-permute-start(bf16[256,384]{1,0:T(8,128)(2,1)} %get-tuple-element.77), channel_id=1, source_target_pairs={{0,32},{32,0},{1,33},{33,1},{2,34},{34,2},{3,35},{35,3},{4,36},{36... | collective-permute-start | bytes 589832 | tf_op jit(solution)/shard_map/ppermute | solution.py:508
  165.5 3.7 %copy-start.18 = (bf16[1024,256]{1,0:T(8,128)(2,1)}, bf16[1024,256]{1,0:T(8,128)(2,1)S(1)}, u32[]{:S(2)}) copy-start(bf16[1024,256]{1,0:T(8,128)(2,1)S(1)} %collective-permute-done.25.down_in.down0) | copy-start | bytes 1572868
  166.1 3.2 %copy-start.15 = (bf16[1040,256]{1,0:T(8,128)(2,1)}, bf16[1040,256]{1,0:T(8,128)(2,1)S(1)}, u32[]{:S(2)}) copy-start(bf16[1040,256]{1,0:T(8,128)(2,1)S(1)} %collective-permute-done.24.up_in.stat_in.up1) | copy-start | bytes 1597444
  169.3 0.7 copy-start.16
  172.2 14.2 %collective-permute-start.26 = (bf16[528,256]{1,0:T(8,128)(2,1)}, bf16[528,256]{1,0:T(8,128)(2,1)S(1)}, u32[]{:S(2)}, u32[]{:S(2)}) collective-permute-start(bf16[528,256]{1,0:T(8,128)(2,1)} %get-tuple-element.85), channel_id=1, source_target_pairs={{0,1},{1,2},{2,3},{3,0},{4,5},{5,6},{6,7},{7,4},{8,9},{9,10},{10,1... | collective-permute-start | bytes 811016 | tf_op jit(solution)/shard_map/ppermute | solution.py:508
  173.7 13.8 %collective-permute-start.27 = (bf16[528,256]{1,0:T(8,128)(2,1)}, bf16[528,256]{1,0:T(8,128)(2,1)S(1)}, u32[]{:S(2)}, u32[]{:S(2)}) collective-permute-start(bf16[528,256]{1,0:T(8,128)(2,1)} %get-tuple-element.86), channel_id=1, source_target_pairs={{0,3},{1,0},{2,1},{3,2},{4,7},{5,4},{6,5},{7,6},{8,11},{9,8},{10,9... | collective-permute-start | bytes 811016 | tf_op jit(solution)/shard_map/ppermute | solution.py:508
  178.6 17.7 %all-to-all-start.3 = ((bf16[4,256,512]{2,1,0:T(8,128)(2,1)}), bf16[4,256,512]{2,1,0:T(8,128)(2,1)S(1)}, u32[]{:S(2)}, u32[]{:S(2)}) async-start(bf16[4,256,512]{2,1,0:T(8,128)(2,1)} %shard_map.71), calls=%async_computation.3 | async-start | bytes 2097152 | tf_op jit(solution)/shard_map/all_to_all | solution.py:589
  186.4 1.1 copy-start.19
  187.5 0.7 copy-start.20
where the time goes:
time: 199 us; the launch traced here: 198 us
  Pallas kernels  69.9 us (35%)
  waiting for transfers between devices  69.6 us (35%)
  starting transfers between devices  49.2 us (25%)
  local copies, waits for them, and re-layouts  8.5 us (4%)
    ppermute x28, waiting for transfers between devices, shift(): return lax.ppermute(x, axis, [(i, (i + by) % n) for i in range(n)])  53.5 us
    ppermute x28, starting transfers between devices, shift(): return lax.ppermute(x, axis, [(i, (i + by) % n) for i in range(n)])  31.4 us
    pallas_call x2, Pallas kernels, norm_halves(): pl.pallas_call(functools.partial(norm_kernel, width, halves, spots, place...  15.4 us
    pallas_call x2, Pallas kernels, project(): pl.pallas_call(functools.partial(project_kernel, offsets, len(sums)), in_...  12.5 us
    all_to_all x1, waiting for transfers between devices, per_device(): lax.all_to_all(proj, 'x', 0, 0, tiled=True).reshape(n_x * rows, 4 * HS)  9.42 us
    pallas_call x1, Pallas kernels, outer(): pl.pallas_call(functools.partial(outer_kernel, tile, spots), in_specs=[pl...  9.34 us
    pallas_call x2, Pallas kernels, unit_rows(): pl.pallas_call(functools.partial(unit_kernel, band=band), grid_spec=pltpu...  7.99 us
    unnamed x42, local copies, waits for them, and re-layouts  7.82 us
  transfers between devices with their start and end apart: 32, of which 17 were waited for; matrix products, arithmetic and copies ran while one was open for 0% of the time, Pallas kernels for 33%

commit v1 on v0

--- a/solution.py
+++ b/solution.py
@@ -290,41 +290,46 @@
     )(ids, grads, proj, *shards, *after)
 
 
-def add_kernel(up_part, up_in, stat_in, down_part, down_in, stat_ref, *refs):
+def add_kernel(up_part, up_in, stat_in, up_direct, down_part, down_in, down_direct, stat_ref, *refs):
     up_out, down_out = refs[-2:]
     half = up_part.shape[0]
-    for part, came, out in ((up_part, up_in, up_out), (down_part, down_in, down_out)):
+    for part, came, direct, out in (
+        (up_part, up_in, up_direct, up_out),
+        (down_part, down_in, down_direct, down_out),
+    ):
         out[:half, :] = (part[...].astype(F32) + came[...].astype(F32)).astype(BF)
-    write_stat(up_out, half, stat_ref[...] + read_stat(stat_in, 0))
-    write_stat(down_out, half, stat_ref[...])
-
-
-def add_messages(up_part, up_in, down_part, down_in, stat, after=()):
+        out[half : 2 * half, :] = direct[...]
+    write_stat(up_out, 2 * half, stat_ref[...] + read_stat(stat_in, 0))
+    write_stat(down_out, 2 * half, stat_ref[...])
+
+
+def add_messages(up_part, up_in, up_direct, down_part, down_in, down_direct, stat, after):
     half, rows = up_part.shape
     block = pl.BlockSpec((half, rows), lambda i: (0, 0))
-    out = pl.BlockSpec((half + 16, rows), lambda i: (0, 0))
-    end = pl.BlockSpec((16, rows), lambda i: (2 * half // 16, 0))
+    out = pl.BlockSpec((2 * half + 16, rows), lambda i: (0, 0))
+    end = pl.BlockSpec((16, rows), lambda i: (half // 16, 0))
     return pl.pallas_call(
         add_kernel,
         grid=(1,),
-        out_shape=(shape(half + 16, rows),) * 2,
-        in_specs=[block, block, end, block, block, pl.BlockSpec((1, rows), lambda i: (0, 0))]
-        + [pl.BlockSpec(memory_space=pl.ANY)] * len(after),
+        out_shape=(shape(2 * half + 16, rows),) * 2,
+        in_specs=[block, block, end]
+        + [block] * 4
+        + [pl.BlockSpec((1, rows), lambda i: (0, 0)), pl.BlockSpec(memory_space=pl.ANY)],
         out_specs=(out, out),
         compiler_params=PARAMS,
         cost_estimate=cost(1, 1),
-    )(up_part, up_in, up_in, down_part, down_in, stat, *after)
-
-
-def finish_kernel(at_ref, own0, own1, up0, up1, down0, down1, tok_ref, root_ref, stat_ref, *refs):
+    )(up_part, up_in, up_in, up_direct, down_part, down_in, down_direct, stat, after)
+
+
+def finish_kernel(at_ref, own0, own1, up, down, tok_ref, root_ref, stat_ref, *refs):
     out_ref = refs[-1]
     half = own0.shape[0]
-    stat = stat_ref[...] + read_stat(up0, half) + read_stat(down1, half)
+    stat = stat_ref[...] + read_stat(up, 2 * half) + read_stat(down, 2 * half)
     stat = jnp.broadcast_to(stat, (HS, stat.shape[1])).T[:, 0:1]
     root = root_ref[...]
     parts = (
-        (own0[...], up0[:half, :], down0[half : 2 * half, :]),
-        (own1[...], up1[half : 2 * half, :], down1[:half, :]),
+        (own0[...], up[:half, :], down[half : 2 * half, :]),
+        (own1[...], up[half : 2 * half, :], down[:half, :]),
     )
     for i, part in enumerate(parts):
         span = slice(i * half, (i + 1) * half)
@@ -566,28 +571,28 @@
 
     up, down, stat = norm_halves(
         ids, grads, proj, shards, places,
-        ((2, 0), (1, 1), (2, 1), (3, 0)),
-        ((0, 0), (0, half), (1, 0), (1, half)),
-        (2 * half + 16, 2 * half),
+        ((2, 0), (2, 1)),
+        ((0, 0), (1, 0)),
+        (half + 16, half),
         width,
     )
     up, down = shift(up, "zh", 1), shift(down, "zh", -1)
-    up_part, down_part, own0, own1, _ = norm_halves(
+    up_part, down_part, up_direct, down_direct, own0, own1, _ = norm_halves(
         ids, grads, proj, shards, places,
-        ((1, 0), (3, 1), (0, 0), (0, 1)),
-        ((0, 0), (1, 0), (2, 0), (3, 0)),
-        (half,) * 4,
+        ((1, 0), (3, 1), (1, 1), (3, 0), (0, 0), (0, 1)),
+        tuple((i, 0) for i in range(6)),
+        (half,) * 6,
         width,
         (stat,),
     )
     part = lax.all_to_all(part, "y", 0, 0, tiled=True).reshape(n_y, 2, w_rows, 3 * HS)
     keep, give = split(ids, part, (own0,))
     came = shift(give, "zl", 1)
-    up_2, down_2 = add_messages(up_part, up, down_part, down, stat, (came,))
+    up_2, down_2 = add_messages(up_part, up, up_direct, down_part, down, down_direct, stat, came)
     last = merge(keep, came, att.reshape(n_x, rows, HS))
     up_2, down_2 = shift(up_2, "zh", 1), shift(down_2, "zh", -1)
     last = lax.all_to_all(last, "x", 0, 0, tiled=True)
-    token_grad = finish(ids, (own0, own1, up_2, up, down, down_2), tokens, root, stat)
+    token_grad = finish(ids, (own0, own1, up_2, down_2), tokens, root, stat)
     weight_grad, attended = unpack(last)
     return attended[None], token_grad[None], weight_grad.transpose(1, 0, 2)
 

time: 199 us -> 198 us (level); the launches traced: 198 us -> 195 us
  waiting for transfers between devices: 69.6 us -> 65.5 us
    all_to_all x1, waiting for transfers between devices: 4.65 us -> 0.01 us  [per_device(): last = lax.all_to_all(last, 'x', 0, 0, tiled=True)]
  transfers between devices with their start and end apart: 32 -> 32, of which waited for: 17 -> 14; matrix products, arithmetic and copies ran while one was open for 0% -> 0% of each run, Pallas kernels for 33% -> 34%
where the time goes in v1:
time: 198 us; the launch traced here: 195 us
  Pallas kernels  70.1 us (35%)
  waiting for transfers between devices  65.5 us (33%)
  starting transfers between devices  49.4 us (25%)
  local copies, waits for them, and re-layouts  8.59 us (4%)
    ppermute x28, waiting for transfers between devices, shift(): return lax.ppermute(x, axis, [(i, (i + by) % n) for i in range(n)])  54.1 us
    ppermute x28, starting transfers between devices, shift(): return lax.ppermute(x, axis, [(i, (i + by) % n) for i in range(n)])  31.4 us
    pallas_call x2, Pallas kernels, norm_halves(): pl.pallas_call(functools.partial(norm_kernel, width, halves, spots, place...  15.2 us
    pallas_call x2, Pallas kernels, project(): pl.pallas_call(functools.partial(project_kernel, offsets, len(sums)), in_...  12.5 us
    all_to_all x1, waiting for transfers between devices, per_device(): lax.all_to_all(proj, 'x', 0, 0, tiled=True).reshape(n_x * rows, 4 * HS)  9.42 us
    pallas_call x1, Pallas kernels, outer(): pl.pallas_call(functools.partial(outer_kernel, tile, spots), in_specs=[pl...  9.34 us
    pallas_call x2, Pallas kernels, unit_rows(): pl.pallas_call(functools.partial(unit_kernel, band=band), grid_spec=pltpu...  7.98 us
    unnamed x42, local copies, waits for them, and re-layouts  7.93 us
  transfers between devices with their start and end apart: 32, of which 14 were waited for; matrix products, arithmetic and copies ran while one was open for 0% of the time, Pallas kernels for 34%

profile of v1, /device:TPU:8, one launch (start us, length us, event | category | flops | bytes accessed | tf_op | source)
XLA Modules:
  0.0 194.5 jit_solution(10571288639619504239)
XLA Ops:
  0.7 1.7 collective-permute-start.7
  2.4 0.7 collective-permute-start.8
  3.1 1.7 collective-permute-start.9
  4.8 0.7 stack.23.at_ref
  5.4 4.2 %shard_map.58 = (f32[256,1]{1,0:T(8,128)}, bf16[256,2048]{1,0:T(8,128)(2,1)}, bf16[1,2048,256]{2,1,0:T(8,128)(2,1)}, bf16[256,2048]{1,0:T(8,128)(2,1)}) custom-call(s32[5]{0:T(128)} %stack.23.at_ref, bf16[256,4096]{1,0:T(8,128)(2,1)} %bitcast.28), custom_call_target="tpu_custom_call" | custom-call | flops 20000000000 | bytes 1 | tf_op jit(solution)/shard_map/pallas_call | solution.py:54
  9.6 1.5 collective-permute-start.1
  11.1 1.7 collective-permute-start.3
  12.8 3.8 %shard_map.59 = (f32[256,1]{1,0:T(8,128)}, bf16[256,2048]{1,0:T(8,128)(2,1)}, bf16[1,2048,256]{2,1,0:T(8,128)(2,1)}) custom-call(s32[5]{0:T(128)} %stack.23.at_ref, bf16[256,4096]{1,0:T(8,128)(2,1)} %collective-permute-done.tok_ref), custom_call_target="tpu_custom_call" | custom-call | flops 20000000000 | bytes 1 | tf_op jit(solution)/shard_map/pallas_call | solution.py:54
  16.6 4.7 %collective-permute-done.7.refs_0_ = bf16[3,256,512]{2,1,0:T(8,128)(2,1)S(1)} collective-permute-done((bf16[3,256,512]{2,1,0:T(8,128)(2,1)}, bf16[3,256,512]{2,1,0:T(8,128)(2,1)S(1)}, u32[]{:S(2)}, u32[]{:S(2)}) %collective-permute-start.7) | collective-permute-done | bytes 786464 | tf_op jit(solution)/shard_map/ppermute | solution.py:513
  21.3 0.9 collective-permute-done.8.refs_1_
  22.2 0.6 collective-permute-done.9.refs_2_
  22.8 0.3 copy-done.10
  23.1 0.6 copy-done.11
  23.7 1.4 collective-permute-start.10
  25.1 1.7 collective-permute-start.11
  26.8 0.6 collective-permute-start.12
  27.4 8.4 %collective-permute-done.1.refs_4_.refs_2_ = bf16[1,2048,256]{2,1,0:T(8,128)(2,1)} collective-permute-done((bf16[1,2048,256]{2,1,0:T(8,128)(2,1)}, bf16[1,2048,256]{2,1,0:T(8,128)(2,1)}, u32[]{:S(2)}, u32[]{:S(2)}) %collective-permute-start.1) | collective-permute-done | bytes 1048608 | tf_op jit(solution)/shard_map/ppermute | solution.py:513
  35.8 1.5 collective-permute-start.4
  37.3 0.5 collective-permute-start.2
  37.8 0.5 copy-done.5
  38.3 6.3 %shard_map.61 = (f32[256,1536]{1,0:T(8,128)}, f32[256,1536]{1,0:T(8,128)}, bf16[4,3,256,512]{3,2,1,0:T(8,128)(2,1)}) custom-call(s32[5]{0:T(128)} %stack.23.at_ref, bf16[256,2048]{1,0:T(8,128)(2,1)} %get-tuple-element.50.mine_ref, bf16[256,2048]{1,0:T(8,128)(2,1)} %get-tuple-element.52.refs_3_.theirs_ref, bf16[3,256,512]{2,1,0:T(8,128)(2,1)} %bitcast.24, ...), custom_call_target="tpu_custom_call" | custom-call | flops 1 | bytes 1 | tf_op jit(solution)/shard_map/pallas_call | solution.py:103
  44.6 0.6 collective-permute-done.12.refs_2_
  45.8 2.0 %shard_map.62 = (bf16[3,256,512]{2,1,0:T(8,128)(2,1)}, bf16[3,256,512]{2,1,0:T(8,128)(2,1)}, bf16[3,256,512]{2,1,0:T(8,128)(2,1)}, bf16[1,256,512]{2,1,0:T(8,128...) custom-call(bf16[3,256,512]{2,1,0:T(8,128)(2,1)} %copy-done.7, ...), custom_call_target="tpu_custom_call", output_to_operand_aliasing={{0}: (0, {}), {1}: (1, {}), {2}: (2, {})} | custom-call | flops 1 | bytes 1 | tf_op jit(solution)/shard_map/pallas_call | solution.py:498
  47.8 1.1 collective-permute-start.13
  48.9 1.7 collective-permute-start.14
  50.9 6.2 %shard_map.63 = (f32[256,1536]{1,0:T(8,128)}, bf16[256,1536]{1,0:T(8,128)(2,1)}, bf16[3,3,256,512]{3,2,1,0:T(8,128)(2,1)}) custom-call(s32[5]{0:T(128)} %stack.23.at_ref, bf16[256,2048]{1,0:T(8,128)(2,1)} %get-tuple-element.50.mine_ref, bf16[256,2048]{1,0:T(8,128)(2,1)} %get-tuple-element.52.refs_3_.theirs_ref, ...), custom_call_target="tpu_custom_call" | custom-call | flops 1 | bytes 1 | tf_op jit(solution)/shard_map/pallas_call | solution.py:103
  57.2 0.4 collective-permute-done.15.refs_2_
  57.6 0.3 copy-done.2
  58.0 0.3 copy-done.4
  58.4 0.5 collective-permute-start.17
  59.0 0.8 collective-permute-done.4.refs_9_.refs_5_
  59.8 2.4 %collective-permute-done.2.refs_8_.refs_3_ = bf16[1,2048,256]{2,1,0:T(8,128)(2,1)S(1)} collective-permute-done((bf16[1,2048,256]{2,1,0:T(8,128)(2,1)}, bf16[1,2048,256]{2,1,0:T(8,128)(2,1)S(1)}, u32[]{:S(2)}, u32[]{:S(2)}) %collective-permute-start.2) | collective-permute-done | bytes 1048608 | tf_op jit(solution)/shard_map/ppermute | solution.py:513
  62.2 3.2 %collective-permute-start.6 = (bf16[1,2048,256]{2,1,0:T(8,128)(2,1)}, bf16[1,2048,256]{2,1,0:T(8,128)(2,1)}, u32[]{:S(2)}, u32[]{:S(2)}) collective-permute-start(bf16[1,2048,256]{2,1,0:T(8,128)(2,1)} %collective-permute-done.4.refs_9_.refs_5_), channel_id=1, source_target_pairs={{0,12},{4,0},{8,4},{12,8},{1,13},{5,1},{9,5},{13,9},{2,14},{6,2},{... | collective-permute-start | bytes 3145736 | tf_op jit(solution)/shard_map/ppermute | solution.py:513
  65.5 0.6 copy-done.13
  66.5 4.3 %shard_map.65 = (bf16[4,256,512]{2,1,0:T(8,128)(2,1)}, bf16[4,3,256,512]{3,2,1,0:T(8,128)(2,1)}, bf16[3,3,256,512]{3,2,1,0:T(8,128)(2,1)}) custom-call(s32[5]{0:T(128)} %stack.23.at_ref, bf16[256,2048]{1,0:T(8,128)(2,1)} %get-tuple-element.50.mine_ref, ...), custom_call_target="tpu_custom_call", output_to_operand_aliasing={{1}: (12, {}), {2}: (13, {})} | custom-call | flops 1 | bytes 1 | tf_op jit(solution)/shard_map/pallas_call | solution.py:141
  70.9 4.2 %all-to-all-start = ((bf16[4,256,512]{2,1,0:T(8,128)(2,1)}), bf16[4,256,512]{2,1,0:T(8,128)(2,1)}, u32[]{:S(2)}, u32[]{:S(2)}) async-start(bf16[4,256,512]{2,1,0:T(8,128)(2,1)} %get-tuple-element.72.p_ref), calls=%async_computation | async-start | bytes 2097152 | tf_op jit(solution)/shard_map/all_to_all | solution.py:558
  75.2 0.5 collective-permute-start.22
  75.7 14.0 %collective-permute-done.5.refs_0_.refs_6_ = bf16[1,2048,256]{2,1,0:T(8,128)(2,1)} collective-permute-done((bf16[1,2048,256]{2,1,0:T(8,128)(2,1)}, bf16[1,2048,256]{2,1,0:T(8,128)(2,1)}, u32[]{:S(2)}, u32[]{:S(2)}) %collective-permute-start.5) | collective-permute-done | bytes 1048608 | tf_op jit(solution)/shard_map/ppermute | solution.py:513
  89.7 9.4 %all-to-all-done = bf16[4,256,512]{2,1,0:T(8,128)(2,1)} async-done(((bf16[4,256,512]{2,1,0:T(8,128)(2,1)}), bf16[4,256,512]{2,1,0:T(8,128)(2,1)}, u32[]{:S(2)}, u32[]{:S(2)}) %all-to-all-start) | async-done | bytes 1048608 | tf_op jit(solution)/shard_map/all_to_all | solution.py:558
  99.2 6.2 %shard_map.66 = (bf16[1024,128]{1,0:T(8,128)(2,1)}, bf16[1024,384]{1,0:T(8,128)(2,1)}) custom-call(bf16[1024,512]{1,0:T(8,128)(2,1)} %bitcast.8.qkv_ref, bf16[1,2048,256]{2,1,0:T(8,128)(2,1)} %collective-permute-done.5.refs_0_.refs_6_, bf16[1,2048,256]{2,1,0:T(8,128)(2,1)} %collective-permute-done.6.refs_1_.refs_7_), custom_call_target="tpu_custom_call" | custom-call | flops 20000000000 | bytes 1 | tf_op jit(solution)/shard_map/pallas_call | solution.py:192
  105.3 4.4 %all-to-all-start.2 = ((bf16[4,256,384]{2,1,0:T(8,128)(2,1)}), bf16[4,256,384]{2,1,0:T(8,128)(2,1)}, u32[]{:S(2)}, u32[]{:S(2)}) async-start(bf16[4,256,384]{2,1,0:T(8,128)(2,1)} %bitcast.19), calls=%async_computation.2 | async-start | bytes 1572864 | tf_op jit(solution)/shard_map/all_to_all | solution.py:569
  109.8 1.7 copy-done
  111.5 9.3 %shard_map.67 = bf16[2048,384]{1,0:T(8,128)(2,1)} custom-call(s32[5]{0:T(128)} %stack.23.at_ref, bf16[1,2048,256]{2,1,0:T(8,128)(2,1)} %get-tuple-element.48.refs_0_, bf16[1,2048,256]{2,1,0:T(8,128)(2,1)} %get-tuple-element.49.refs_1_, bf16[1,2048,256]{2,1,0:T(8,128)(2,1)} %collective-permute-done.1.refs_4_.refs_2_, bf16[1,2048,256]{2,1,0:T(8,128)(2,1)} %copy-done.6, ...), custom_call_target="tpu_custom_call" | custom-call | flops 1 | bytes 1 | tf_op jit(solution)/shard_map/pallas_call | solution.py:396
  120.8 2.0 %all-to-all-done.2.g_ref = bf16[4,256,384]{2,1,0:T(8,128)(2,1)} async-done(((bf16[4,256,384]{2,1,0:T(8,128)(2,1)}), bf16[4,256,384]{2,1,0:T(8,128)(2,1)}, u32[]{:S(2)}, u32[]{:S(2)}) %all-to-all-start.2) | async-done | bytes 786464 | tf_op jit(solution)/shard_map/all_to_all | solution.py:569
  122.8 5.7 %all-to-all-start.1 = ((bf16[4,512,384]{2,1,0:T(8,128)(2,1)}), bf16[4,512,384]{2,1,0:T(8,128)(2,1)S(1)}, u32[]{:S(2)}, u32[]{:S(2)}) async-start(bf16[4,512,384]{2,1,0:T(8,128)(2,1)} %bitcast.16), calls=%async_computation.1 | async-start | bytes 3145728 | tf_op jit(solution)/shard_map/all_to_all | solution.py:588
  128.5 5.6 %shard_map.68 = (bf16[528,256]{1,0:T(8,128)(2,1)}, bf16[512,256]{1,0:T(8,128)(2,1)}, f32[1,256]{1,0:T(1,128)}) custom-call(s32[5]{0:T(128)} %stack.23.at_ref, bf16[4,256,384]{2,1,0:T(8,128)(2,1)} %all-to-all-done.2.g_ref, bf16[4,256,512]{2,1,0:T(8,128)(2,1)} %get-tuple-element.72.p_ref, bf16[1,256,512]{2,1,0:T(8,128)(2,1)} %get-tuple-element.67.refs_0_, ...), custom_call_target="tpu_custom_call" | custom-call | flops 1 | bytes 1 | tf_op jit(solution)/shard_map/pallas_call | solution.py:277
  134.1 3.4 %collective-permute-start.24 = (bf16[528,256]{1,0:T(8,128)(2,1)}, bf16[528,256]{1,0:T(8,128)(2,1)S(1)}, u32[]{:S(2)}, u32[]{:S(2)}) collective-permute-start(bf16[528,256]{1,0:T(8,128)(2,1)} %get-tuple-element.84), channel_id=1, source_target_pairs={{0,1},{1,2},{2,3},{3,0},{4,5},{5,6},{6,7},{7,4},{8,9},{9,10},{10,1... | collective-permute-start | bytes 811016 | tf_op jit(solution)/shard_map/ppermute | solution.py:513
  137.5 2.2 %collective-permute-start.25 = (bf16[512,256]{1,0:T(8,128)(2,1)}, bf16[512,256]{1,0:T(8,128)(2,1)S(1)}, u32[]{:S(2)}, u32[]{:S(2)}) collective-permute-start(bf16[512,256]{1,0:T(8,128)(2,1)} %get-tuple-element.87), channel_id=1, source_target_pairs={{0,3},{1,0},{2,1},{3,2},{4,7},{5,4},{6,5},{7,6},{8,11},{9,8},{10,9... | collective-permute-start | bytes 786440 | tf_op jit(solution)/shard_map/ppermute | solution.py:513
  139.7 9.7 %shard_map.69 = (bf16[512,256]{1,0:T(8,128)(2,1)}, bf16[512,256]{1,0:T(8,128)(2,1)}, bf16[512,256]{1,0:T(8,128)(2,1)}, bf16[512,256]{1,0:T(8,128)(2,1)}, bf16[51...) custom-call(s32[5]{0:T(128)} %stack.23.at_ref, bf16[4,256,384]{2,1,0:T(8,128)(2,1)} %all-to-all-done.2.g_ref, ...), custom_call_target="tpu_custom_call" | custom-call | flops 1 | bytes 1 | tf_op jit(solution)/shard_map/pallas_call | solution.py:277
  149.4 1.1 copy-done.1
  150.5 2.3 %shard_map.70 = (f32[256,384]{1,0:T(8,128)}, bf16[256,384]{1,0:T(8,128)(2,1)}) custom-call(s32[5]{0:T(128)} %stack.23.at_ref, bf16[4,2,256,384]{3,2,1,0:T(8,128)(2,1)} %bitcast.17, bf16[512,256]{1,0:T(8,128)(2,1)} %get-tuple-element.77.refs_0_.own0), custom_call_target="tpu_custom_call" | custom-call | flops 1 | bytes 1 | tf_op jit(solution)/shard_map/pallas_call | solution.py:424
  152.8 1.0 collective-permute-start.23
  153.8 4.9 %collective-permute-done.23.came_ref.refs_0_ = bf16[256,384]{1,0:T(8,128)(2,1)S(1)} collective-permute-done((bf16[256,384]{1,0:T(8,128)(2,1)}, bf16[256,384]{1,0:T(8,128)(2,1)S(1)}, u32[]{:S(2)}, u32[]{:S(2)}) %collective-permute-start.23) | collective-permute-done | bytes 196640 | tf_op jit(solution)/shard_map/ppermute | solution.py:513
  158.7 0.7 copy-done.16
  159.4 2.7 %shard_map.73 = (bf16[1040,256]{1,0:T(8,128)(2,1)}, bf16[1040,256]{1,0:T(8,128)(2,1)}) custom-call(bf16[512,256]{1,0:T(8,128)(2,1)} %get-tuple-element.83.up_part, bf16[528,256]{1,0:T(8,128)(2,1)} %copy-done.15, bf16[528,256]{1,0:T(8,128)(2,1)} %copy-done.15, bf16[512,256]{1,0:T(8,128)(2,1)} %get-tuple-element.85.up_direct, ...), custom_call_target="tpu_custom_call" | custom-call | flops 1 | bytes 1 | tf_op jit(solution)/shard_map/pallas_call | solution.py:311
  162.1 1.5 collective-permute-start.26
  163.5 2.7 %collective-permute-start.27 = (bf16[1040,256]{1,0:T(8,128)(2,1)}, bf16[1040,256]{1,0:T(8,128)(2,1)S(1)}, u32[]{:S(2)}, u32[]{:S(2)}) collective-permute-start(bf16[1040,256]{1,0:T(8,128)(2,1)} %get-tuple-element.90), channel_id=1, source_target_pairs={{0,3},{1,0},{2,1},{3,2},{4,7},{5,4},{6,5},{7,6},{8,11},{9,8},{10,9... | collective-permute-start | bytes 1597448 | tf_op jit(solution)/shard_map/ppermute | solution.py:513
  166.2 2.2 %shard_map.71 = bf16[4,256,512]{2,1,0:T(8,128)(2,1)} custom-call(f32[256,384]{1,0:T(8,128)} %get-tuple-element.78.keep_ref, bf16[256,384]{1,0:T(8,128)(2,1)} %copy-done.16, bf16[4,256,128]{2,1,0:T(8,128)(2,1)} %bitcast.26), custom_call_target="tpu_custom_call" | custom-call | flops 1 | bytes 1 | tf_op jit(solution)/shard_map/pallas_call | solution.py:448
  168.4 3.6 %all-to-all-start.3 = ((bf16[4,256,512]{2,1,0:T(8,128)(2,1)}), bf16[4,256,512]{2,1,0:T(8,128)(2,1)S(1)}, u32[]{:S(2)}, u32[]{:S(2)}) async-start(bf16[4,256,512]{2,1,0:T(8,128)(2,1)} %shard_map.71), calls=%async_computation.3 | async-start | bytes 2097152 | tf_op jit(solution)/shard_map/all_to_all | solution.py:594
  172.1 8.9 %collective-permute-done.26.up = bf16[1040,256]{1,0:T(8,128)(2,1)S(1)} collective-permute-done((bf16[1040,256]{1,0:T(8,128)(2,1)}, bf16[1040,256]{1,0:T(8,128)(2,1)S(1)}, u32[]{:S(2)}, u32[]{:S(2)}) %collective-permute-start.26) | collective-permute-done | bytes 532512 | tf_op jit(solution)/shard_map/ppermute | solution.py:513
  181.0 7.5 %collective-permute-done.27.down = bf16[1040,256]{1,0:T(8,128)(2,1)S(1)} collective-permute-done((bf16[1040,256]{1,0:T(8,128)(2,1)}, bf16[1040,256]{1,0:T(8,128)(2,1)S(1)}, u32[]{:S(2)}, u32[]{:S(2)}) %collective-permute-start.27) | collective-permute-done | bytes 532512 | tf_op jit(solution)/shard_map/ppermute | solution.py:513
  188.5 0.8 copy-done.20
  189.3 3.3 %shard_map.74 = bf16[256,1024]{1,0:T(8,128)(2,1)} custom-call(s32[5]{0:T(128)} %stack.23.at_ref, bf16[512,256]{1,0:T(8,128)(2,1)} %get-tuple-element.77.refs_0_.own0, bf16[512,256]{1,0:T(8,128)(2,1)} %get-tuple-element.82.own1, bf16[1040,256]{1,0:T(8,128)(2,1)} %copy-done.19, bf16[1040,256]{1,0:T(8,128)(2,1)} %copy-done.20, bf16[256,4096]{1,0:T(8,128)(2,1)} %bitcast.29, ...), custom_call_target="tpu_custom_call" | custom-call | flops 20000000000 | bytes 1 | tf_op jit(solution)/shard_map/pallas_call | solution.py:346
  192.7 1.9 shard_map.72
  (60 shorter events, 1.7 us)
Async XLA Ops:
  0.6 10.4 %collective-permute-start = (bf16[256,4096]{1,0:T(8,128)(2,1)}, bf16[256,4096]{1,0:T(8,128)(2,1)}, u32[]{:S(2)}, u32[]{:S(2)}) collective-permute-start(bf16[256,4096]{1,0:T(8,128)(2,1)} %bitcast.27), channel_id=1, source_target_pairs={{0,16},{16,0},{1,17},{17,1},{2,18},{18,2},{3,19},{19,3},{4,20},{20... | collective-permute-start | bytes 6291464 | tf_op jit(solution)/shard_map/ppermute | solution.py:513
  0.7 20.6 %collective-permute-start.7 = (bf16[3,256,512]{2,1,0:T(8,128)(2,1)}, bf16[3,256,512]{2,1,0:T(8,128)(2,1)S(1)}, u32[]{:S(2)}, u32[]{:S(2)}) collective-permute-start(bf16[3,256,512]{2,1,0:T(8,128)(2,1)} %bitcast.21), channel_id=1, source_target_pairs={{0,64},{64,128},{128,192},{192,0},{1,65},{65,129},{129,193},{193,1... | collective-permute-start | bytes 2359304 | tf_op jit(solution)/shard_map/ppermute | solution.py:513
  2.4 19.8 %collective-permute-start.8 = (bf16[3,256,512]{2,1,0:T(8,128)(2,1)}, bf16[3,256,512]{2,1,0:T(8,128)(2,1)S(1)}, u32[]{:S(2)}, u32[]{:S(2)}) collective-permute-start(bf16[3,256,512]{2,1,0:T(8,128)(2,1)} %bitcast.22), channel_id=1, source_target_pairs={{0,192},{64,0},{128,64},{192,128},{1,193},{65,1},{129,65},{193,129... | collective-permute-start | bytes 2359304 | tf_op jit(solution)/shard_map/ppermute | solution.py:513
  3.1 19.7 %collective-permute-start.9 = (bf16[3,256,512]{2,1,0:T(8,128)(2,1)}, bf16[3,256,512]{2,1,0:T(8,128)(2,1)S(1)}, u32[]{:S(2)}, u32[]{:S(2)}) collective-permute-start(bf16[3,256,512]{2,1,0:T(8,128)(2,1)} %bitcast.23), channel_id=1, source_target_pairs={{0,32},{32,0},{1,33},{33,1},{2,34},{34,2},{3,35},{35,3},{4,36},{36... | collective-permute-start | bytes 2359304 | tf_op jit(solution)/shard_map/ppermute | solution.py:513
  9.6 26.2 %collective-permute-start.1 = (bf16[1,2048,256]{2,1,0:T(8,128)(2,1)}, bf16[1,2048,256]{2,1,0:T(8,128)(2,1)}, u32[]{:S(2)}, u32[]{:S(2)}) collective-permute-start(bf16[1,2048,256]{2,1,0:T(8,128)(2,1)} %get-tuple-element.48.refs_0_), channel_id=1, source_target_pairs={{0,4},{4,8},{8,12},{12,0},{1,5},{5,9},{9,13},{13,1},{2,6},{6,10},{... | collective-permute-start | bytes 3145736 | tf_op jit(solution)/shard_map/ppermute | solution.py:513
  11.1 26.2 %collective-permute-start.3 = (bf16[1,2048,256]{2,1,0:T(8,128)(2,1)}, bf16[1,2048,256]{2,1,0:T(8,128)(2,1)S(1)}, u32[]{:S(2)}, u32[]{:S(2)}) collective-permute-start(bf16[1,2048,256]{2,1,0:T(8,128)(2,1)} %get-tuple-element.48.refs_0_), channel_id=1, source_target_pairs={{0,12},{4,0},{8,4},{12,8},{1,13},{5,1},{9,5},{13,9},{2,14},{6,2},{... | collective-permute-start | bytes 3145736 | tf_op jit(solution)/shard_map/ppermute | solution.py:513
  21.3 1.5 copy-start.9
  22.2 0.9 copy-start.10
  22.8 0.9 copy-start.11
  23.7 20.9 %collective-permute-start.10 = (bf16[3,256,512]{2,1,0:T(8,128)(2,1)}, bf16[3,256,512]{2,1,0:T(8,128)(2,1)S(1)}, u32[]{:S(2)}, u32[]{:S(2)}) collective-permute-start(bf16[3,256,512]{2,1,0:T(8,128)(2,1)} %get-tuple-element.53.refs_1_), channel_id=1, source_target_pairs={{0,64},{64,128},{128,192},{192,0},{1,65},{65,129},{129,193},{193,1... | collective-permute-start | bytes 2359304 | tf_op jit(solution)/shard_map/ppermute | solution.py:513
  25.1 19.5 %collective-permute-start.11 = (bf16[3,256,512]{2,1,0:T(8,128)(2,1)}, bf16[3,256,512]{2,1,0:T(8,128)(2,1)S(1)}, u32[]{:S(2)}, u32[]{:S(2)}) collective-permute-start(bf16[3,256,512]{2,1,0:T(8,128)(2,1)} %get-tuple-element.53.refs_1_), channel_id=1, source_target_pairs={{0,32},{32,0},{1,33},{33,1},{2,34},{34,2},{3,35},{35,3},{4,36},{36... | collective-permute-start | bytes 2359304 | tf_op jit(solution)/shard_map/ppermute | solution.py:513
  26.8 18.4 %collective-permute-start.12 = (bf16[3,256,512]{2,1,0:T(8,128)(2,1)}, bf16[3,256,512]{2,1,0:T(8,128)(2,1)}, u32[]{:S(2)}, u32[]{:S(2)}) collective-permute-start(bf16[3,256,512]{2,1,0:T(8,128)(2,1)} %get-tuple-element.54.refs_3_), channel_id=1, source_target_pairs={{0,192},{64,0},{128,64},{192,128},{1,193},{65,1},{129,65},{193,129... | collective-permute-start | bytes 2359304 | tf_op jit(solution)/shard_map/ppermute | solution.py:513
  35.8 24.1 %collective-permute-start.4 = (bf16[1,2048,256]{2,1,0:T(8,128)(2,1)}, bf16[1,2048,256]{2,1,0:T(8,128)(2,1)}, u32[]{:S(2)}, u32[]{:S(2)}) collective-permute-start(bf16[1,2048,256]{2,1,0:T(8,128)(2,1)} %get-tuple-element.49.refs_1_), channel_id=1, source_target_pairs={{0,12},{4,0},{8,4},{12,8},{1,13},{5,1},{9,5},{13,9},{2,14},{6,2},{... | collective-permute-start | bytes 3145736 | tf_op jit(solution)/shard_map/ppermute | solution.py:513
  37.3 1.0 copy-start.5
  37.3 24.9 %collective-permute-start.2 = (bf16[1,2048,256]{2,1,0:T(8,128)(2,1)}, bf16[1,2048,256]{2,1,0:T(8,128)(2,1)S(1)}, u32[]{:S(2)}, u32[]{:S(2)}) collective-permute-start(bf16[1,2048,256]{2,1,0:T(8,128)(2,1)} %get-tuple-element.49.refs_1_), channel_id=1, source_target_pairs={{0,4},{4,8},{8,12},{12,0},{1,5},{5,9},{9,13},{13,1},{2,6},{6,10},{... | collective-permute-start | bytes 3145736 | tf_op jit(solution)/shard_map/ppermute | solution.py:513
  44.6 0.9 copy-start.7
  44.6 1.1 copy-start.8
  47.8 9.4 %collective-permute-start.13 = (bf16[1,256,512]{2,1,0:T(8,128)(2,1)}, bf16[1,256,512]{2,1,0:T(8,128)(2,1)S(1)}, u32[]{:S(2)}, u32[]{:S(2)}) collective-permute-start(bf16[1,256,512]{2,1,0:T(8,128)(2,1)} %get-tuple-element.62), channel_id=1, source_target_pairs={{0,32},{32,0},{1,33},{33,1},{2,34},{34,2},{3,35},{35,3},{4,36},{36... | collective-permute-start | bytes 786440 | tf_op jit(solution)/shard_map/ppermute | solution.py:513
  48.9 8.3 %collective-permute-start.14 = (bf16[1,256,512]{2,1,0:T(8,128)(2,1)}, bf16[1,256,512]{2,1,0:T(8,128)(2,1)S(1)}, u32[]{:S(2)}, u32[]{:S(2)}) collective-permute-start(bf16[1,256,512]{2,1,0:T(8,128)(2,1)} %get-tuple-element.63), channel_id=1, source_target_pairs={{0,64},{64,128},{128,192},{192,0},{1,65},{65,129},{129,193},{193,1... | collective-permute-start | bytes 786440 | tf_op jit(solution)/shard_map/ppermute | solution.py:513
  50.6 6.9 %collective-permute-start.15 = (bf16[1,256,512]{2,1,0:T(8,128)(2,1)}, bf16[1,256,512]{2,1,0:T(8,128)(2,1)S(1)}, u32[]{:S(2)}, u32[]{:S(2)}) collective-permute-start(bf16[1,256,512]{2,1,0:T(8,128)(2,1)} %get-tuple-element.64), channel_id=1, source_target_pairs={{0,192},{64,0},{128,64},{192,128},{1,193},{65,1},{129,65},{193,129... | collective-permute-start | bytes 786440 | tf_op jit(solution)/shard_map/ppermute | solution.py:513
  57.2 0.7 copy-start.2
  57.2 0.8 copy-start.3
  57.6 0.7 copy-start.4
  58.3 7.1 %collective-permute-start.16 = (bf16[256,1536]{1,0:T(8,128)(2,1)}, bf16[256,1536]{1,0:T(8,128)(2,1)S(1)}, u32[]{:S(2)}, u32[]{:S(2)}) collective-permute-start(bf16[256,1536]{1,0:T(8,128)(2,1)} %get-tuple-element.66), channel_id=1, source_target_pairs={{0,16},{16,0},{1,17},{17,1},{2,18},{18,2},{3,19},{19,3},{4,20},{20... | collective-permute-start | bytes 2359304 | tf_op jit(solution)/shard_map/ppermute | solution.py:513
  58.4 3.8 %collective-permute-start.17 = (bf16[1,256,512]{2,1,0:T(8,128)(2,1)}, bf16[1,256,512]{2,1,0:T(8,128)(2,1)S(1)}, u32[]{:S(2)}, u32[]{:S(2)}) collective-permute-start(bf16[1,256,512]{2,1,0:T(8,128)(2,1)} %get-tuple-element.67.refs_0_), channel_id=1, source_target_pairs={{0,16},{16,0},{1,17},{17,1},{2,18},{18,2},{3,19},{19,3},{4,20},{20... | collective-permute-start | bytes 786440 | tf_op jit(solution)/shard_map/ppermute | solution.py:513
  58.9 6.5 %collective-permute-start.18 = (bf16[1,256,512]{2,1,0:T(8,128)(2,1)}, bf16[1,256,512]{2,1,0:T(8,128)(2,1)S(1)}, u32[]{:S(2)}, u32[]{:S(2)}) collective-permute-start(bf16[1,256,512]{2,1,0:T(8,128)(2,1)} %get-tuple-element.68.refs_1_), channel_id=1, source_target_pairs={{0,16},{16,0},{1,17},{17,1},{2,18},{18,2},{3,19},{19,3},{4,20},{20... | collective-permute-start | bytes 786440 | tf_op jit(solution)/shard_map/ppermute | solution.py:513
  59.8 5.6 %collective-permute-start.19 = (bf16[1,256,512]{2,1,0:T(8,128)(2,1)}, bf16[1,256,512]{2,1,0:T(8,128)(2,1)S(1)}, u32[]{:S(2)}, u32[]{:S(2)}) collective-permute-start(bf16[1,256,512]{2,1,0:T(8,128)(2,1)} %get-tuple-element.69.refs_2_), channel_id=1, source_target_pairs={{0,16},{16,0},{1,17},{17,1},{2,18},{18,2},{3,19},{19,3},{4,20},{20... | collective-permute-start | bytes 786440 | tf_op jit(solution)/shard_map/ppermute | solution.py:513
  62.2 3.3 %copy-start.6 = (bf16[1,2048,256]{2,1,0:T(8,128)(2,1)}, bf16[1,2048,256]{2,1,0:T(8,128)(2,1)S(1)}, u32[]{:S(2)}) copy-start(bf16[1,2048,256]{2,1,0:T(8,128)(2,1)S(1)} %collective-permute-done.2.refs_8_.refs_3_) | copy-start | bytes 3145732
  62.2 27.5 %collective-permute-start.5 = (bf16[1,2048,256]{2,1,0:T(8,128)(2,1)}, bf16[1,2048,256]{2,1,0:T(8,128)(2,1)}, u32[]{:S(2)}, u32[]{:S(2)}) collective-permute-start(bf16[1,2048,256]{2,1,0:T(8,128)(2,1)} %collective-permute-done.1.refs_4_.refs_2_), channel_id=1, source_target_pairs={{0,4},{4,8},{8,12},{12,0},{1,5},{5,9},{9,13},{13,1},{2,6},{6,10},{... | collective-permute-start | bytes 3145736 | tf_op jit(solution)/shard_map/ppermute | solution.py:513
  62.2 3.3 %copy-start.12 = (bf16[1,256,512]{2,1,0:T(8,128)(2,1)}, bf16[1,256,512]{2,1,0:T(8,128)(2,1)S(1)}, u32[]{:S(2)}) copy-start(bf16[1,256,512]{2,1,0:T(8,128)(2,1)S(1)} %collective-permute-done.17.refs_3_) | copy-start | bytes 786436
  62.2 27.5 %collective-permute-start.6 = (bf16[1,2048,256]{2,1,0:T(8,128)(2,1)}, bf16[1,2048,256]{2,1,0:T(8,128)(2,1)}, u32[]{:S(2)}, u32[]{:S(2)}) collective-permute-start(bf16[1,2048,256]{2,1,0:T(8,128)(2,1)} %collective-permute-done.4.refs_9_.refs_5_), channel_id=1, source_target_pairs={{0,12},{4,0},{8,4},{12,8},{1,13},{5,1},{9,5},{13,9},{2,14},{6,2},{... | collective-permute-start | bytes 3145736 | tf_op jit(solution)/shard_map/ppermute | solution.py:513
  65.5 0.7 copy-start.13
  65.5 0.8 copy-start.14
  65.5 1.0 copy-start.17
  70.9 28.3 %all-to-all-start = ((bf16[4,256,512]{2,1,0:T(8,128)(2,1)}), bf16[4,256,512]{2,1,0:T(8,128)(2,1)}, u32[]{:S(2)}, u32[]{:S(2)}) async-start(bf16[4,256,512]{2,1,0:T(8,128)(2,1)} %get-tuple-element.72.p_ref), calls=%async_computation | async-start | bytes 2097152 | tf_op jit(solution)/shard_map/all_to_all | solution.py:558
  75.1 34.7 %collective-permute-start.21 = (bf16[4,3,256,512]{3,2,1,0:T(8,128)(2,1)}, bf16[4,3,256,512]{3,2,1,0:T(8,128)(2,1)S(1)}, u32[]{:S(2)}, u32[]{:S(2)}) collective-permute-start(bf16[4,3,256,512]{3,2,1,0:T(8,128)(2,1)} %get-tuple-element.74.refs_6_), channel_id=1, source_target_pairs={{0,16},{16,0},{1,17},{17,1},{2,18},{18,2},{3,19},{19,3},{4,20},{20... | collective-permute-start | bytes 9437192 | tf_op jit(solution)/shard_map/ppermute | solution.py:513
  75.2 34.6 %collective-permute-start.22 = (bf16[3,3,256,512]{3,2,1,0:T(8,128)(2,1)}, bf16[3,3,256,512]{3,2,1,0:T(8,128)(2,1)}, u32[]{:S(2)}, u32[]{:S(2)}) collective-permute-start(bf16[3,3,256,512]{3,2,1,0:T(8,128)(2,1)} %get-tuple-element.75.refs_8_), channel_id=1, source_target_pairs={{0,16},{16,0},{1,17},{17,1},{2,18},{18,2},{3,19},{19,3},{4,20},{20... | collective-permute-start | bytes 7077896 | tf_op jit(solution)/shard_map/ppermute | solution.py:513
  105.3 4.4 %collective-permute-start.20 = (bf16[4,256,384]{2,1,0:T(8,128)(2,1)}, bf16[4,256,384]{2,1,0:T(8,128)(2,1)}, u32[]{:S(2)}, u32[]{:S(2)}) collective-permute-start(bf16[4,256,384]{2,1,0:T(8,128)(2,1)} %bitcast.18), channel_id=1, source_target_pairs={{0,16},{16,0},{1,17},{17,1},{2,18},{18,2},{3,19},{19,3},{4,20},{20... | collective-permute-start | bytes 2359304 | tf_op jit(solution)/shard_map/ppermute | solution.py:513
  105.3 17.5 %all-to-all-start.2 = ((bf16[4,256,384]{2,1,0:T(8,128)(2,1)}), bf16[4,256,384]{2,1,0:T(8,128)(2,1)}, u32[]{:S(2)}, u32[]{:S(2)}) async-start(bf16[4,256,384]{2,1,0:T(8,128)(2,1)} %bitcast.19), calls=%async_computation.2 | async-start | bytes 1572864 | tf_op jit(solution)/shard_map/all_to_all | solution.py:569
  109.8 1.7 copy-start
  122.8 26.5 %all-to-all-start.1 = ((bf16[4,512,384]{2,1,0:T(8,128)(2,1)}), bf16[4,512,384]{2,1,0:T(8,128)(2,1)S(1)}, u32[]{:S(2)}, u32[]{:S(2)}) async-start(bf16[4,512,384]{2,1,0:T(8,128)(2,1)} %bitcast.16), calls=%async_computation.1 | async-start | bytes 3145728 | tf_op jit(solution)/shard_map/all_to_all | solution.py:588
  134.1 19.7 %collective-permute-start.24 = (bf16[528,256]{1,0:T(8,128)(2,1)}, bf16[528,256]{1,0:T(8,128)(2,1)S(1)}, u32[]{:S(2)}, u32[]{:S(2)}) collective-permute-start(bf16[528,256]{1,0:T(8,128)(2,1)} %get-tuple-element.84), channel_id=1, source_target_pairs={{0,1},{1,2},{2,3},{3,0},{4,5},{5,6},{6,7},{7,4},{8,9},{9,10},{10,1... | collective-permute-start | bytes 811016 | tf_op jit(solution)/shard_map/ppermute | solution.py:513
  137.5 16.3 %collective-permute-start.25 = (bf16[512,256]{1,0:T(8,128)(2,1)}, bf16[512,256]{1,0:T(8,128)(2,1)S(1)}, u32[]{:S(2)}, u32[]{:S(2)}) collective-permute-start(bf16[512,256]{1,0:T(8,128)(2,1)} %get-tuple-element.87), channel_id=1, source_target_pairs={{0,3},{1,0},{2,1},{3,2},{4,7},{5,4},{6,5},{7,6},{8,11},{9,8},{10,9... | collective-permute-start | bytes 786440 | tf_op jit(solution)/shard_map/ppermute | solution.py:513
  149.4 1.1 copy-start.1
  152.8 5.9 %collective-permute-start.23 = (bf16[256,384]{1,0:T(8,128)(2,1)}, bf16[256,384]{1,0:T(8,128)(2,1)S(1)}, u32[]{:S(2)}, u32[]{:S(2)}) collective-permute-start(bf16[256,384]{1,0:T(8,128)(2,1)} %get-tuple-element.79), channel_id=1, source_target_pairs={{0,32},{32,0},{1,33},{33,1},{2,34},{34,2},{3,35},{35,3},{4,36},{36... | collective-permute-start | bytes 589832 | tf_op jit(solution)/shard_map/ppermute | solution.py:513
  153.8 4.9 %copy-start.18 = (bf16[512,256]{1,0:T(8,128)(2,1)}, bf16[512,256]{1,0:T(8,128)(2,1)S(1)}, u32[]{:S(2)}) copy-start(bf16[512,256]{1,0:T(8,128)(2,1)S(1)} %collective-permute-done.25.down_in) | copy-start | bytes 786436
  153.8 4.9 %copy-start.15 = (bf16[528,256]{1,0:T(8,128)(2,1)}, bf16[528,256]{1,0:T(8,128)(2,1)S(1)}, u32[]{:S(2)}) copy-start(bf16[528,256]{1,0:T(8,128)(2,1)S(1)} %collective-permute-done.24.up_in.stat_in) | copy-start | bytes 811012
  158.7 0.7 copy-start.16
  162.1 19.0 %collective-permute-start.26 = (bf16[1040,256]{1,0:T(8,128)(2,1)}, bf16[1040,256]{1,0:T(8,128)(2,1)S(1)}, u32[]{:S(2)}, u32[]{:S(2)}) collective-permute-start(bf16[1040,256]{1,0:T(8,128)(2,1)} %get-tuple-element.89), channel_id=1, source_target_pairs={{0,1},{1,2},{2,3},{3,0},{4,5},{5,6},{6,7},{7,4},{8,9},{9,10},{10,1... | collective-permute-start | bytes 1597448 | tf_op jit(solution)/shard_map/ppermute | solution.py:513
  163.5 25.0 %collective-permute-start.27 = (bf16[1040,256]{1,0:T(8,128)(2,1)}, bf16[1040,256]{1,0:T(8,128)(2,1)S(1)}, u32[]{:S(2)}, u32[]{:S(2)}) collective-permute-start(bf16[1040,256]{1,0:T(8,128)(2,1)} %get-tuple-element.90), channel_id=1, source_target_pairs={{0,3},{1,0},{2,1},{3,2},{4,7},{5,4},{6,5},{7,6},{8,11},{9,8},{10,9... | collective-permute-start | bytes 1597448 | tf_op jit(solution)/shard_map/ppermute | solution.py:513
  168.4 24.2 %all-to-all-start.3 = ((bf16[4,256,512]{2,1,0:T(8,128)(2,1)}), bf16[4,256,512]{2,1,0:T(8,128)(2,1)S(1)}, u32[]{:S(2)}, u32[]{:S(2)}) async-start(bf16[4,256,512]{2,1,0:T(8,128)(2,1)} %shard_map.71), calls=%async_computation.3 | async-start | bytes 2097152 | tf_op jit(solution)/shard_map/all_to_all | solution.py:594
  181.0 7.5 %copy-start.19 = (bf16[1040,256]{1,0:T(8,128)(2,1)}, bf16[1040,256]{1,0:T(8,128)(2,1)S(1)}, u32[]{:S(2)}) copy-start(bf16[1040,256]{1,0:T(8,128)(2,1)S(1)} %collective-permute-done.26.up) | copy-start | bytes 1597444
  188.5 0.8 copy-start.20

commit v2 on v1

--- a/solution.py
+++ b/solution.py
@@ -577,19 +577,23 @@
         width,
     )
     up, down = shift(up, "zh", 1), shift(down, "zh", -1)
-    up_part, down_part, up_direct, down_direct, own0, own1, _ = norm_halves(
+    up_part, down_part, up_direct, down_direct, _ = norm_halves(
         ids, grads, proj, shards, places,
-        ((1, 0), (3, 1), (1, 1), (3, 0), (0, 0), (0, 1)),
-        tuple((i, 0) for i in range(6)),
-        (half,) * 6,
+        ((1, 0), (3, 1), (1, 1), (3, 0)),
+        tuple((i, 0) for i in range(4)),
+        (half,) * 4,
         width,
         (stat,),
     )
     part = lax.all_to_all(part, "y", 0, 0, tiled=True).reshape(n_y, 2, w_rows, 3 * HS)
-    keep, give = split(ids, part, (own0,))
+    keep, give = split(ids, part, (up_part,))
     came = shift(give, "zl", 1)
     up_2, down_2 = add_messages(up_part, up, up_direct, down_part, down, down_direct, stat, came)
-    last = merge(keep, came, att.reshape(n_x, rows, HS))
+    own0, own1, _ = norm_halves(
+        ids, grads, proj, shards, places, ((0, 0), (0, 1)), ((0, 0), (1, 0)), (half, half), width,
+        (up_2,),
+    )
+    last = merge(keep, came, att.reshape(n_x, rows, HS), (own0,))
     up_2, down_2 = shift(up_2, "zh", 1), shift(down_2, "zh", -1)
     last = lax.all_to_all(last, "x", 0, 0, tiled=True)
     token_grad = finish(ids, (own0, own1, up_2, down_2), tokens, root, stat)

time: 198 us -> 201 us (1.015)
  starting transfers between devices: 49.4 us -> 53.1 us
  Pallas kernels: 70.1 us -> 73.6 us
  waiting for transfers between devices: 65.5 us -> 62 us
    ppermute x28, waiting for transfers between devices: 54.1 us -> 50.1 us  [shift(): return lax.ppermute(x, axis, [(i, (i + by) % n) for i in range(n)])]
    pallas_call x2 -> x3, Pallas kernels: 15.2 us -> 18.8 us  [norm_halves(): pl.pallas_call(functools.partial(norm_kernel, width, halves, spots, place...]
    ppermute x28, starting transfers between devices: 31.4 us -> 33.6 us  [shift(): return lax.ppermute(x, axis, [(i, (i + by) % n) for i in range(n)])]
  transfers between devices with their start and end apart: 32 -> 32, of which waited for: 14 -> 15; matrix products, arithmetic and copies ran while one was open for 0% -> 0% of each run, Pallas kernels for 34% -> 35%
where the time goes in v2:
time: 201 us; the launch traced here: 198 us
  Pallas kernels  73.6 us (37%)
  waiting for transfers between devices  62 us (31%)
  starting transfers between devices  53.1 us (26%)
  local copies, waits for them, and re-layouts  8.22 us (4%)
    ppermute x28, waiting for transfers between devices, shift(): return lax.ppermute(x, axis, [(i, (i + by) % n) for i in range(n)])  50.1 us
    ppermute x28, starting transfers between devices, shift(): return lax.ppermute(x, axis, [(i, (i + by) % n) for i in range(n)])  33.6 us
    pallas_call x3, Pallas kernels, norm_halves(): pl.pallas_call(functools.partial(norm_kernel, width, halves, spots, place...  18.8 us
    pallas_call x2, Pallas kernels, project(): pl.pallas_call(functools.partial(project_kernel, offsets, len(sums)), in_...  12.5 us
    all_to_all x1, waiting for transfers between devices, per_device(): lax.all_to_all(proj, 'x', 0, 0, tiled=True).reshape(n_x * rows, 4 * HS)  9.62 us
    pallas_call x1, Pallas kernels, outer(): pl.pallas_call(functools.partial(outer_kernel, tile, spots), in_specs=[pl...  9.34 us
    pallas_call x2, Pallas kernels, unit_rows(): pl.pallas_call(functools.partial(unit_kernel, band=band), grid_spec=pltpu...  7.91 us
    unnamed x42, local copies, waits for them, and re-layouts  7.58 us
  transfers between devices with their start and end apart: 32, of which 15 were waited for; matrix products, arithmetic and copies ran while one was open for 0% of the time, Pallas kernels for 35%

profile of v2, /device:TPU:8, one launch (start us, length us, event | category | flops | bytes accessed | tf_op | source)
XLA Modules:
  0.0 197.8 jit_solution(18297117592269919435)
XLA Ops:
  0.7 2.0 %collective-permute-start.9 = (bf16[3,256,512]{2,1,0:T(8,128)(2,1)}, bf16[3,256,512]{2,1,0:T(8,128)(2,1)S(1)}, u32[]{:S(2)}, u32[]{:S(2)}) collective-permute-start(bf16[3,256,512]{2,1,0:T(8,128)(2,1)} %bitcast.21), channel_id=1, source_target_pairs={{0,32},{32,0},{1,33},{33,1},{2,34},{34,2},{3,35},{35,3},{4,36},{36... | collective-permute-start | bytes 2359304 | tf_op jit(solution)/shard_map/ppermute | solution.py:513
  2.7 0.4 collective-permute-start.8
  3.2 1.6 collective-permute-start.7
  4.8 0.6 stack.23.at_ref
  5.4 4.1 %shard_map.58 = (f32[256,1]{1,0:T(8,128)}, bf16[256,2048]{1,0:T(8,128)(2,1)}, bf16[1,2048,256]{2,1,0:T(8,128)(2,1)}, bf16[256,2048]{1,0:T(8,128)(2,1)}) custom-call(s32[5]{0:T(128)} %stack.23.at_ref, bf16[256,4096]{1,0:T(8,128)(2,1)} %bitcast.28), custom_call_target="tpu_custom_call" | custom-call | flops 20000000000 | bytes 1 | tf_op jit(solution)/shard_map/pallas_call | solution.py:54
  9.5 2.8 %collective-permute-start.3 = (bf16[1,2048,256]{2,1,0:T(8,128)(2,1)}, bf16[1,2048,256]{2,1,0:T(8,128)(2,1)S(1)}, u32[]{:S(2)}, u32[]{:S(2)}) collective-permute-start(bf16[1,2048,256]{2,1,0:T(8,128)(2,1)} %get-tuple-element.48.refs_0_), channel_id=1, source_target_pairs={{0,12},{4,0},{8,4},{12,8},{1,13},{5,1},{9,5},{13,9},{2,14},{6,2},{... | collective-permute-start | bytes 3145736 | tf_op jit(solution)/shard_map/ppermute | solution.py:513
  12.2 3.8 %shard_map.59 = (f32[256,1]{1,0:T(8,128)}, bf16[256,2048]{1,0:T(8,128)(2,1)}, bf16[1,2048,256]{2,1,0:T(8,128)(2,1)}) custom-call(s32[5]{0:T(128)} %stack.23.at_ref, bf16[256,4096]{1,0:T(8,128)(2,1)} %collective-permute-done.tok_ref), custom_call_target="tpu_custom_call" | custom-call | flops 20000000000 | bytes 1 | tf_op jit(solution)/shard_map/pallas_call | solution.py:54
  16.1 5.0 %collective-permute-done.9.refs_2_ = bf16[3,256,512]{2,1,0:T(8,128)(2,1)S(1)} collective-permute-done((bf16[3,256,512]{2,1,0:T(8,128)(2,1)}, bf16[3,256,512]{2,1,0:T(8,128)(2,1)S(1)}, u32[]{:S(2)}, u32[]{:S(2)}) %collective-permute-start.9) | collective-permute-done | bytes 786464 | tf_op jit(solution)/shard_map/ppermute | solution.py:513
  21.1 1.5 collective-permute-done.8.refs_1_
  22.5 1.5 collective-permute-done.7.refs_0_
  24.0 0.9 copy-done.14
  24.9 3.0 %collective-permute-start.12 = (bf16[3,256,512]{2,1,0:T(8,128)(2,1)}, bf16[3,256,512]{2,1,0:T(8,128)(2,1)S(1)}, u32[]{:S(2)}, u32[]{:S(2)}) collective-permute-start(bf16[3,256,512]{2,1,0:T(8,128)(2,1)} %get-tuple-element.54.refs_3_), channel_id=1, source_target_pairs={{0,192},{64,0},{128,64},{192,128},{1,193},{65,1},{129,65},{193,129... | collective-permute-start | bytes 2359304 | tf_op jit(solution)/shard_map/ppermute | solution.py:513
  27.9 0.3 collective-permute-start.11
  28.2 6.5 %collective-permute-done.3.refs_5_.refs_4_ = bf16[1,2048,256]{2,1,0:T(8,128)(2,1)S(1)} collective-permute-done((bf16[1,2048,256]{2,1,0:T(8,128)(2,1)}, bf16[1,2048,256]{2,1,0:T(8,128)(2,1)S(1)}, u32[]{:S(2)}, u32[]{:S(2)}) %collective-permute-start.3) | collective-permute-done | bytes 1048608 | tf_op jit(solution)/shard_map/ppermute | solution.py:513
  34.7 3.6 %collective-permute-start.4 = (bf16[1,2048,256]{2,1,0:T(8,128)(2,1)}, bf16[1,2048,256]{2,1,0:T(8,128)(2,1)}, u32[]{:S(2)}, u32[]{:S(2)}) collective-permute-start(bf16[1,2048,256]{2,1,0:T(8,128)(2,1)} %get-tuple-element.49.refs_1_), channel_id=1, source_target_pairs={{0,12},{4,0},{8,4},{12,8},{1,13},{5,1},{9,5},{13,9},{2,14},{6,2},{... | collective-permute-start | bytes 3145736 | tf_op jit(solution)/shard_map/ppermute | solution.py:513
  38.3 6.4 %shard_map.61 = (f32[256,1536]{1,0:T(8,128)}, f32[256,1536]{1,0:T(8,128)}, bf16[4,3,256,512]{3,2,1,0:T(8,128)(2,1)}) custom-call(s32[5]{0:T(128)} %stack.23.at_ref, bf16[256,2048]{1,0:T(8,128)(2,1)} %get-tuple-element.50.mine_ref, bf16[256,2048]{1,0:T(8,128)(2,1)} %get-tuple-element.52.refs_3_.theirs_ref, bf16[3,256,512]{2,1,0:T(8,128)(2,1)} %bitcast.24, ...), custom_call_target="tpu_custom_call" | custom-call | flops 1 | bytes 1 | tf_op jit(solution)/shard_map/pallas_call | solution.py:103
  44.7 1.7 collective-permute-done.11.refs_1_
  46.4 0.3 collective-permute-done.10.refs_0_
  46.7 0.6 copy-done.11
  47.3 2.0 %shard_map.62 = (bf16[3,256,512]{2,1,0:T(8,128)(2,1)}, bf16[3,256,512]{2,1,0:T(8,128)(2,1)}, bf16[3,256,512]{2,1,0:T(8,128)(2,1)}, bf16[1,256,512]{2,1,0:T(8,128...) custom-call(bf16[3,256,512]{2,1,0:T(8,128)(2,1)} %collective-permute, ...), custom_call_target="tpu_custom_call", output_to_operand_aliasing={{0}: (0, {}), {1}: (1, {}), {2}: (2, {})} | custom-call | flops 1 | bytes 1 | tf_op jit(solution)/shard_map/pallas_call | solution.py:498
  49.3 1.1 collective-permute-start.13
  50.4 0.3 collective-permute-start.14
  50.7 1.8 collective-permute-start.15
  52.5 6.2 %shard_map.63 = (f32[256,1536]{1,0:T(8,128)}, bf16[256,1536]{1,0:T(8,128)(2,1)}, bf16[3,3,256,512]{3,2,1,0:T(8,128)(2,1)}) custom-call(s32[5]{0:T(128)} %stack.23.at_ref, bf16[256,2048]{1,0:T(8,128)(2,1)} %get-tuple-element.50.mine_ref, bf16[256,2048]{1,0:T(8,128)(2,1)} %get-tuple-element.52.refs_3_.theirs_ref, ...), custom_call_target="tpu_custom_call" | custom-call | flops 1 | bytes 1 | tf_op jit(solution)/shard_map/pallas_call | solution.py:103
  58.8 0.7 copy-done.1
  59.4 0.1 copy-done.2
  59.7 0.5 collective-permute-start.17
  60.3 0.4 collective-permute-start.19
  60.7 2.5 %collective-permute-done.2.refs_8_.refs_3_ = bf16[1,2048,256]{2,1,0:T(8,128)(2,1)S(1)} collective-permute-done((bf16[1,2048,256]{2,1,0:T(8,128)(2,1)}, bf16[1,2048,256]{2,1,0:T(8,128)(2,1)S(1)}, u32[]{:S(2)}, u32[]{:S(2)}) %collective-permute-start.2) | collective-permute-done | bytes 1048608 | tf_op jit(solution)/shard_map/ppermute | solution.py:513
  63.2 3.2 %collective-permute-start.6 = (bf16[1,2048,256]{2,1,0:T(8,128)(2,1)}, bf16[1,2048,256]{2,1,0:T(8,128)(2,1)}, u32[]{:S(2)}, u32[]{:S(2)}) collective-permute-start(bf16[1,2048,256]{2,1,0:T(8,128)(2,1)} %collective-permute-done.4.refs_9_.refs_5_), channel_id=1, source_target_pairs={{0,12},{4,0},{8,4},{12,8},{1,13},{5,1},{9,5},{13,9},{2,14},{6,2},{... | collective-permute-start | bytes 3145736 | tf_op jit(solution)/shard_map/ppermute | solution.py:513
  66.5 0.6 copy-done.6
  67.2 0.3 copy-done.17
  67.5 4.4 %shard_map.65 = (bf16[4,256,512]{2,1,0:T(8,128)(2,1)}, bf16[4,3,256,512]{3,2,1,0:T(8,128)(2,1)}, bf16[3,3,256,512]{3,2,1,0:T(8,128)(2,1)}) custom-call(s32[5]{0:T(128)} %stack.23.at_ref, bf16[256,2048]{1,0:T(8,128)(2,1)} %get-tuple-element.50.mine_ref, ...), custom_call_target="tpu_custom_call", output_to_operand_aliasing={{1}: (12, {}), {2}: (13, {})} | custom-call | flops 1 | bytes 1 | tf_op jit(solution)/shard_map/pallas_call | solution.py:141
  72.0 4.2 %all-to-all-start = ((bf16[4,256,512]{2,1,0:T(8,128)(2,1)}), bf16[4,256,512]{2,1,0:T(8,128)(2,1)}, u32[]{:S(2)}, u32[]{:S(2)}) async-start(bf16[4,256,512]{2,1,0:T(8,128)(2,1)} %get-tuple-element.72.p_ref), calls=%async_computation | async-start | bytes 2097152 | tf_op jit(solution)/shard_map/all_to_all | solution.py:558
  76.3 0.5 collective-permute-start.22
  76.8 13.8 %collective-permute-done.5.refs_0_.refs_6_ = bf16[1,2048,256]{2,1,0:T(8,128)(2,1)} collective-permute-done((bf16[1,2048,256]{2,1,0:T(8,128)(2,1)}, bf16[1,2048,256]{2,1,0:T(8,128)(2,1)}, u32[]{:S(2)}, u32[]{:S(2)}) %collective-permute-start.5) | collective-permute-done | bytes 1048608 | tf_op jit(solution)/shard_map/ppermute | solution.py:513
  90.6 9.6 %all-to-all-done = bf16[4,256,512]{2,1,0:T(8,128)(2,1)} async-done(((bf16[4,256,512]{2,1,0:T(8,128)(2,1)}), bf16[4,256,512]{2,1,0:T(8,128)(2,1)}, u32[]{:S(2)}, u32[]{:S(2)}) %all-to-all-start) | async-done | bytes 1048608 | tf_op jit(solution)/shard_map/all_to_all | solution.py:558
  100.2 6.2 %shard_map.66 = (bf16[1024,128]{1,0:T(8,128)(2,1)}, bf16[1024,384]{1,0:T(8,128)(2,1)}) custom-call(bf16[1024,512]{1,0:T(8,128)(2,1)} %bitcast.8.qkv_ref, bf16[1,2048,256]{2,1,0:T(8,128)(2,1)} %collective-permute-done.5.refs_0_.refs_6_, bf16[1,2048,256]{2,1,0:T(8,128)(2,1)} %collective-permute-done.6.refs_1_.refs_7_), custom_call_target="tpu_custom_call" | custom-call | flops 20000000000 | bytes 1 | tf_op jit(solution)/shard_map/pallas_call | solution.py:192
  106.4 4.4 %all-to-all-start.2 = ((bf16[4,256,384]{2,1,0:T(8,128)(2,1)}), bf16[4,256,384]{2,1,0:T(8,128)(2,1)}, u32[]{:S(2)}, u32[]{:S(2)}) async-start(bf16[4,256,384]{2,1,0:T(8,128)(2,1)} %bitcast.19), calls=%async_computation.2 | async-start | bytes 1572864 | tf_op jit(solution)/shard_map/all_to_all | solution.py:569
  110.8 1.6 copy-done
  112.4 9.3 %shard_map.67 = bf16[2048,384]{1,0:T(8,128)(2,1)} custom-call(s32[5]{0:T(128)} %stack.23.at_ref, bf16[1,2048,256]{2,1,0:T(8,128)(2,1)} %get-tuple-element.48.refs_0_, bf16[1,2048,256]{2,1,0:T(8,128)(2,1)} %get-tuple-element.49.refs_1_, bf16[1,2048,256]{2,1,0:T(8,128)(2,1)} %collective-permute-done.1.refs_4_.refs_2_, bf16[1,2048,256]{2,1,0:T(8,128)(2,1)} %copy-done.9, ...), custom_call_target="tpu_custom_call" | custom-call | flops 1 | bytes 1 | tf_op jit(solution)/shard_map/pallas_call | solution.py:396
  121.8 2.1 %all-to-all-done.2.g_ref = bf16[4,256,384]{2,1,0:T(8,128)(2,1)} async-done(((bf16[4,256,384]{2,1,0:T(8,128)(2,1)}), bf16[4,256,384]{2,1,0:T(8,128)(2,1)}, u32[]{:S(2)}, u32[]{:S(2)}) %all-to-all-start.2) | async-done | bytes 786464 | tf_op jit(solution)/shard_map/all_to_all | solution.py:569
  123.9 6.8 %all-to-all-start.1 = ((bf16[4,512,384]{2,1,0:T(8,128)(2,1)}), bf16[4,512,384]{2,1,0:T(8,128)(2,1)S(1)}, u32[]{:S(2)}, u32[]{:S(2)}) async-start(bf16[4,512,384]{2,1,0:T(8,128)(2,1)} %bitcast.16), calls=%async_computation.1 | async-start | bytes 3145728 | tf_op jit(solution)/shard_map/all_to_all | solution.py:588
  130.6 5.6 %shard_map.68 = (bf16[528,256]{1,0:T(8,128)(2,1)}, bf16[512,256]{1,0:T(8,128)(2,1)}, f32[1,256]{1,0:T(1,128)}) custom-call(s32[5]{0:T(128)} %stack.23.at_ref, bf16[4,256,384]{2,1,0:T(8,128)(2,1)} %all-to-all-done.2.g_ref, bf16[4,256,512]{2,1,0:T(8,128)(2,1)} %get-tuple-element.72.p_ref, bf16[1,256,512]{2,1,0:T(8,128)(2,1)} %get-tuple-element.67.refs_0_, ...), custom_call_target="tpu_custom_call" | custom-call | flops 1 | bytes 1 | tf_op jit(solution)/shard_map/pallas_call | solution.py:277
  136.2 3.4 %collective-permute-start.24 = (bf16[528,256]{1,0:T(8,128)(2,1)}, bf16[528,256]{1,0:T(8,128)(2,1)S(1)}, u32[]{:S(2)}, u32[]{:S(2)}) collective-permute-start(bf16[528,256]{1,0:T(8,128)(2,1)} %get-tuple-element.81), channel_id=1, source_target_pairs={{0,1},{1,2},{2,3},{3,0},{4,5},{5,6},{6,7},{7,4},{8,9},{9,10},{10,1... | collective-permute-start | bytes 811016 | tf_op jit(solution)/shard_map/ppermute | solution.py:513
  139.6 2.2 %collective-permute-start.25 = (bf16[512,256]{1,0:T(8,128)(2,1)}, bf16[512,256]{1,0:T(8,128)(2,1)S(1)}, u32[]{:S(2)}, u32[]{:S(2)}) collective-permute-start(bf16[512,256]{1,0:T(8,128)(2,1)} %get-tuple-element.84), channel_id=1, source_target_pairs={{0,3},{1,0},{2,1},{3,2},{4,7},{5,4},{6,5},{7,6},{8,11},{9,8},{10,9... | collective-permute-start | bytes 786440 | tf_op jit(solution)/shard_map/ppermute | solution.py:513
  141.8 7.6 %shard_map.69 = (bf16[512,256]{1,0:T(8,128)(2,1)}, bf16[512,256]{1,0:T(8,128)(2,1)}, bf16[512,256]{1,0:T(8,128)(2,1)}, bf16[512,256]{1,0:T(8,128)(2,1)}, f32[1,256]{1,0:T(1,128)}) custom-call(s32[5]{0:T(128)} %stack.23.at_ref, bf16[4,256,384]{2,1,0:T(8,128)(2,1)} %all-to-all-done.2.g_ref, bf16[4,256,512]{2,1,0:T(8,128)(2,1)} %get-tuple-element.72.p_ref, ...), custom_call_target="tpu_custom_call" | custom-call | flops 1 | bytes 1 | tf_op jit(solution)/shard_map/pallas_call | solution.py:277
  149.4 0.2 all-to-all-done.1
  149.6 1.1 copy-done.4
  150.8 2.3 %shard_map.70 = (f32[256,384]{1,0:T(8,128)}, bf16[256,384]{1,0:T(8,128)(2,1)}) custom-call(s32[5]{0:T(128)} %stack.23.at_ref, bf16[4,2,256,384]{3,2,1,0:T(8,128)(2,1)} %bitcast.17, bf16[512,256]{1,0:T(8,128)(2,1)} %get-tuple-element.77.refs_0_.up_part), custom_call_target="tpu_custom_call" | custom-call | flops 1 | bytes 1 | tf_op jit(solution)/shard_map/pallas_call | solution.py:424
  153.1 0.8 collective-permute-start.23
  153.8 0.4 collective-permute-done.25.down_in
  154.2 4.7 %collective-permute-done.23.refs_0_.came_ref = bf16[256,384]{1,0:T(8,128)(2,1)S(1)} collective-permute-done((bf16[256,384]{1,0:T(8,128)(2,1)}, bf16[256,384]{1,0:T(8,128)(2,1)S(1)}, u32[]{:S(2)}, u32[]{:S(2)}) %collective-permute-start.23) | collective-permute-done | bytes 196640 | tf_op jit(solution)/shard_map/ppermute | solution.py:513
  159.0 0.7 copy-done.16
  159.6 2.6 %shard_map.71 = (bf16[1040,256]{1,0:T(8,128)(2,1)}, bf16[1040,256]{1,0:T(8,128)(2,1)}) custom-call(bf16[512,256]{1,0:T(8,128)(2,1)} %get-tuple-element.77.refs_0_.up_part, bf16[528,256]{1,0:T(8,128)(2,1)} %copy-done.15, bf16[528,256]{1,0:T(8,128)(2,1)} %copy-done.15, bf16[512,256]{1,0:T(8,128)(2,1)} %get-tuple-element.82.up_direct, ...), custom_call_target="tpu_custom_call" | custom-call | flops 1 | bytes 1 | tf_op jit(solution)/shard_map/pallas_call | solution.py:311
  162.3 5.4 %collective-permute-start.27 = (bf16[1040,256]{1,0:T(8,128)(2,1)}, bf16[1040,256]{1,0:T(8,128)(2,1)S(1)}, u32[]{:S(2)}, u32[]{:S(2)}) collective-permute-start(bf16[1040,256]{1,0:T(8,128)(2,1)} %get-tuple-element.90), channel_id=1, source_target_pairs={{0,3},{1,0},{2,1},{3,2},{4,7},{5,4},{6,5},{7,6},{8,11},{9,8},{10,9... | collective-permute-start | bytes 1597448 | tf_op jit(solution)/shard_map/ppermute | solution.py:513
  167.7 5.6 %shard_map.72 = (bf16[512,256]{1,0:T(8,128)(2,1)}, bf16[512,256]{1,0:T(8,128)(2,1)}, f32[1,256]{1,0:T(1,128)}) custom-call(s32[5]{0:T(128)} %stack.23.at_ref, bf16[4,256,384]{2,1,0:T(8,128)(2,1)} %all-to-all-done.2.g_ref, bf16[4,256,512]{2,1,0:T(8,128)(2,1)} %get-tuple-element.72.p_ref, bf16[1,256,512]{2,1,0:T(8,128)(2,1)} %get-tuple-element.67.refs_0_, ...), custom_call_target="tpu_custom_call" | custom-call | flops 1 | bytes 1 | tf_op jit(solution)/shard_map/pallas_call | solution.py:277
  173.3 2.2 %shard_map.73 = bf16[4,256,512]{2,1,0:T(8,128)(2,1)} custom-call(f32[256,384]{1,0:T(8,128)} %get-tuple-element.78.keep_ref, bf16[256,384]{1,0:T(8,128)(2,1)} %copy-done.16, bf16[4,256,128]{2,1,0:T(8,128)(2,1)} %bitcast.26, bf16[512,256]{1,0:T(8,128)(2,1)} %get-tuple-element.87.refs_0_.own0), custom_call_target="tpu_custom_call" | custom-call | flops 1 | bytes 1 | tf_op jit(solution)/shard_map/pallas_call | solution.py:448
  175.5 4.1 %all-to-all-start.3 = ((bf16[4,256,512]{2,1,0:T(8,128)(2,1)}), bf16[4,256,512]{2,1,0:T(8,128)(2,1)S(1)}, u32[]{:S(2)}, u32[]{:S(2)}) async-start(bf16[4,256,512]{2,1,0:T(8,128)(2,1)} %shard_map.73), calls=%async_computation.3 | async-start | bytes 2097152 | tf_op jit(solution)/shard_map/all_to_all | solution.py:598
  179.6 7.0 %collective-permute-done.27.down = bf16[1040,256]{1,0:T(8,128)(2,1)S(1)} collective-permute-done((bf16[1040,256]{1,0:T(8,128)(2,1)}, bf16[1040,256]{1,0:T(8,128)(2,1)S(1)}, u32[]{:S(2)}, u32[]{:S(2)}) %collective-permute-start.27) | collective-permute-done | bytes 532512 | tf_op jit(solution)/shard_map/ppermute | solution.py:513
  186.6 5.3 %collective-permute-done.26.up = bf16[1040,256]{1,0:T(8,128)(2,1)S(1)} collective-permute-done((bf16[1040,256]{1,0:T(8,128)(2,1)}, bf16[1040,256]{1,0:T(8,128)(2,1)S(1)}, u32[]{:S(2)}, u32[]{:S(2)}) %collective-permute-start.26) | collective-permute-done | bytes 532512 | tf_op jit(solution)/shard_map/ppermute | solution.py:513
  191.9 0.8 copy-done.20
  192.7 3.3 %shard_map.75 = bf16[256,1024]{1,0:T(8,128)(2,1)} custom-call(s32[5]{0:T(128)} %stack.23.at_ref, bf16[512,256]{1,0:T(8,128)(2,1)} %get-tuple-element.87.refs_0_.own0, bf16[512,256]{1,0:T(8,128)(2,1)} %get-tuple-element.89.own1, bf16[1040,256]{1,0:T(8,128)(2,1)} %copy-done.20, bf16[1040,256]{1,0:T(8,128)(2,1)} %copy-done.19, bf16[256,4096]{1,0:T(8,128)(2,1)} %bitcast.29, ...), custom_call_target="tpu_custom_call" | custom-call | flops 20000000000 | bytes 1 | tf_op jit(solution)/shard_map/pallas_call | solution.py:346
  196.0 1.9 shard_map.74
  (61 shorter events, 0.7 us)
Async XLA Ops:
  0.6 11.6 %collective-permute-start = (bf16[256,4096]{1,0:T(8,128)(2,1)}, bf16[256,4096]{1,0:T(8,128)(2,1)}, u32[]{:S(2)}, u32[]{:S(2)}) collective-permute-start(bf16[256,4096]{1,0:T(8,128)(2,1)} %bitcast.27), channel_id=1, source_target_pairs={{0,16},{16,0},{1,17},{17,1},{2,18},{18,2},{3,19},{19,3},{4,20},{20... | collective-permute-start | bytes 6291464 | tf_op jit(solution)/shard_map/ppermute | solution.py:513
  0.7 20.3 %collective-permute-start.9 = (bf16[3,256,512]{2,1,0:T(8,128)(2,1)}, bf16[3,256,512]{2,1,0:T(8,128)(2,1)S(1)}, u32[]{:S(2)}, u32[]{:S(2)}) collective-permute-start(bf16[3,256,512]{2,1,0:T(8,128)(2,1)} %bitcast.21), channel_id=1, source_target_pairs={{0,32},{32,0},{1,33},{33,1},{2,34},{34,2},{3,35},{35,3},{4,36},{36... | collective-permute-start | bytes 2359304 | tf_op jit(solution)/shard_map/ppermute | solution.py:513
  2.7 19.8 %collective-permute-start.8 = (bf16[3,256,512]{2,1,0:T(8,128)(2,1)}, bf16[3,256,512]{2,1,0:T(8,128)(2,1)S(1)}, u32[]{:S(2)}, u32[]{:S(2)}) collective-permute-start(bf16[3,256,512]{2,1,0:T(8,128)(2,1)} %bitcast.22), channel_id=1, source_target_pairs={{0,192},{64,0},{128,64},{192,128},{1,193},{65,1},{129,65},{193,129... | collective-permute-start | bytes 2359304 | tf_op jit(solution)/shard_map/ppermute | solution.py:513
  3.2 20.8 %collective-permute-start.7 = (bf16[3,256,512]{2,1,0:T(8,128)(2,1)}, bf16[3,256,512]{2,1,0:T(8,128)(2,1)S(1)}, u32[]{:S(2)}, u32[]{:S(2)}) collective-permute-start(bf16[3,256,512]{2,1,0:T(8,128)(2,1)} %bitcast.23), channel_id=1, source_target_pairs={{0,64},{64,128},{128,192},{192,0},{1,65},{65,129},{129,193},{193,1... | collective-permute-start | bytes 2359304 | tf_op jit(solution)/shard_map/ppermute | solution.py:513
  9.5 25.3 %collective-permute-start.3 = (bf16[1,2048,256]{2,1,0:T(8,128)(2,1)}, bf16[1,2048,256]{2,1,0:T(8,128)(2,1)S(1)}, u32[]{:S(2)}, u32[]{:S(2)}) collective-permute-start(bf16[1,2048,256]{2,1,0:T(8,128)(2,1)} %get-tuple-element.48.refs_0_), channel_id=1, source_target_pairs={{0,12},{4,0},{8,4},{12,8},{1,13},{5,1},{9,5},{13,9},{2,14},{6,2},{... | collective-permute-start | bytes 3145736 | tf_op jit(solution)/shard_map/ppermute | solution.py:513
  12.2 26.1 %collective-permute-start.1 = (bf16[1,2048,256]{2,1,0:T(8,128)(2,1)}, bf16[1,2048,256]{2,1,0:T(8,128)(2,1)}, u32[]{:S(2)}, u32[]{:S(2)}) collective-permute-start(bf16[1,2048,256]{2,1,0:T(8,128)(2,1)} %get-tuple-element.48.refs_0_), channel_id=1, source_target_pairs={{0,4},{4,8},{8,12},{12,0},{1,5},{5,9},{9,13},{13,1},{2,6},{6,10},{... | collective-permute-start | bytes 3145736 | tf_op jit(solution)/shard_map/ppermute | solution.py:513
  21.1 3.0 %copy-start.12 = (bf16[3,256,512]{2,1,0:T(8,128)(2,1)}, bf16[3,256,512]{2,1,0:T(8,128)(2,1)S(1)}, u32[]{:S(2)}) copy-start(bf16[3,256,512]{2,1,0:T(8,128)(2,1)S(1)} %collective-permute-done.9.refs_2_) | copy-start | bytes 2359300
  22.5 1.5 copy-start.13
  24.0 0.9 copy-start.14
  24.9 19.8 %collective-permute-start.12 = (bf16[3,256,512]{2,1,0:T(8,128)(2,1)}, bf16[3,256,512]{2,1,0:T(8,128)(2,1)S(1)}, u32[]{:S(2)}, u32[]{:S(2)}) collective-permute-start(bf16[3,256,512]{2,1,0:T(8,128)(2,1)} %get-tuple-element.54.refs_3_), channel_id=1, source_target_pairs={{0,192},{64,0},{128,64},{192,128},{1,193},{65,1},{129,65},{193,129... | collective-permute-start | bytes 2359304 | tf_op jit(solution)/shard_map/ppermute | solution.py:513
  27.9 18.5 %collective-permute-start.11 = (bf16[3,256,512]{2,1,0:T(8,128)(2,1)}, bf16[3,256,512]{2,1,0:T(8,128)(2,1)S(1)}, u32[]{:S(2)}, u32[]{:S(2)}) collective-permute-start(bf16[3,256,512]{2,1,0:T(8,128)(2,1)} %get-tuple-element.53.refs_1_), channel_id=1, source_target_pairs={{0,32},{32,0},{1,33},{33,1},{2,34},{34,2},{3,35},{35,3},{4,36},{36... | collective-permute-start | bytes 2359304 | tf_op jit(solution)/shard_map/ppermute | solution.py:513
  28.2 18.5 %collective-permute-start.10 = (bf16[3,256,512]{2,1,0:T(8,128)(2,1)}, bf16[3,256,512]{2,1,0:T(8,128)(2,1)}, u32[]{:S(2)}, u32[]{:S(2)}) collective-permute-start(bf16[3,256,512]{2,1,0:T(8,128)(2,1)} %get-tuple-element.53.refs_1_), channel_id=1, source_target_pairs={{0,64},{64,128},{128,192},{192,0},{1,65},{65,129},{129,193},{193,1... | collective-permute-start | bytes 2359304 | tf_op jit(solution)/shard_map/ppermute | solution.py:513
  34.7 3.6 %copy-start.8 = (bf16[1,2048,256]{2,1,0:T(8,128)(2,1)}, bf16[1,2048,256]{2,1,0:T(8,128)(2,1)S(1)}, u32[]{:S(2)}) copy-start(bf16[1,2048,256]{2,1,0:T(8,128)(2,1)S(1)} %collective-permute-done.3.refs_5_.refs_4_) | copy-start | bytes 3145732
  34.7 25.6 %collective-permute-start.4 = (bf16[1,2048,256]{2,1,0:T(8,128)(2,1)}, bf16[1,2048,256]{2,1,0:T(8,128)(2,1)}, u32[]{:S(2)}, u32[]{:S(2)}) collective-permute-start(bf16[1,2048,256]{2,1,0:T(8,128)(2,1)} %get-tuple-element.49.refs_1_), channel_id=1, source_target_pairs={{0,12},{4,0},{8,4},{12,8},{1,13},{5,1},{9,5},{13,9},{2,14},{6,2},{... | collective-permute-start | bytes 3145736 | tf_op jit(solution)/shard_map/ppermute | solution.py:513
  38.3 24.9 %collective-permute-start.2 = (bf16[1,2048,256]{2,1,0:T(8,128)(2,1)}, bf16[1,2048,256]{2,1,0:T(8,128)(2,1)S(1)}, u32[]{:S(2)}, u32[]{:S(2)}) collective-permute-start(bf16[1,2048,256]{2,1,0:T(8,128)(2,1)} %get-tuple-element.49.refs_1_), channel_id=1, source_target_pairs={{0,4},{4,8},{8,12},{12,0},{1,5},{5,9},{9,13},{13,1},{2,6},{6,10},{... | collective-permute-start | bytes 3145736 | tf_op jit(solution)/shard_map/ppermute | solution.py:513
  44.7 1.9 copy-start.10
  46.4 0.9 copy-start.11
  49.3 9.4 %collective-permute-start.13 = (bf16[1,256,512]{2,1,0:T(8,128)(2,1)}, bf16[1,256,512]{2,1,0:T(8,128)(2,1)S(1)}, u32[]{:S(2)}, u32[]{:S(2)}) collective-permute-start(bf16[1,256,512]{2,1,0:T(8,128)(2,1)} %get-tuple-element.62), channel_id=1, source_target_pairs={{0,32},{32,0},{1,33},{33,1},{2,34},{34,2},{3,35},{35,3},{4,36},{36... | collective-permute-start | bytes 786440 | tf_op jit(solution)/shard_map/ppermute | solution.py:513
  50.4 8.4 %collective-permute-start.14 = (bf16[1,256,512]{2,1,0:T(8,128)(2,1)}, bf16[1,256,512]{2,1,0:T(8,128)(2,1)S(1)}, u32[]{:S(2)}, u32[]{:S(2)}) collective-permute-start(bf16[1,256,512]{2,1,0:T(8,128)(2,1)} %get-tuple-element.63), channel_id=1, source_target_pairs={{0,64},{64,128},{128,192},{192,0},{1,65},{65,129},{129,193},{193,1... | collective-permute-start | bytes 786440 | tf_op jit(solution)/shard_map/ppermute | solution.py:513
  50.7 8.1 %collective-permute-start.15 = (bf16[1,256,512]{2,1,0:T(8,128)(2,1)}, bf16[1,256,512]{2,1,0:T(8,128)(2,1)S(1)}, u32[]{:S(2)}, u32[]{:S(2)}) collective-permute-start(bf16[1,256,512]{2,1,0:T(8,128)(2,1)} %get-tuple-element.64), channel_id=1, source_target_pairs={{0,192},{64,0},{128,64},{192,128},{1,193},{65,1},{129,65},{193,129... | collective-permute-start | bytes 786440 | tf_op jit(solution)/shard_map/ppermute | solution.py:513
  58.7 0.7 copy-start.1
  58.7 0.8 copy-start.2
  58.8 0.8 copy-start.3
  59.6 6.9 %collective-permute-start.16 = (bf16[256,1536]{1,0:T(8,128)(2,1)}, bf16[256,1536]{1,0:T(8,128)(2,1)S(1)}, u32[]{:S(2)}, u32[]{:S(2)}) collective-permute-start(bf16[256,1536]{1,0:T(8,128)(2,1)} %get-tuple-element.66), channel_id=1, source_target_pairs={{0,16},{16,0},{1,17},{17,1},{2,18},{18,2},{3,19},{19,3},{4,20},{20... | collective-permute-start | bytes 2359304 | tf_op jit(solution)/shard_map/ppermute | solution.py:513
  59.7 3.5 %collective-permute-start.17 = (bf16[1,256,512]{2,1,0:T(8,128)(2,1)}, bf16[1,256,512]{2,1,0:T(8,128)(2,1)S(1)}, u32[]{:S(2)}, u32[]{:S(2)}) collective-permute-start(bf16[1,256,512]{2,1,0:T(8,128)(2,1)} %get-tuple-element.67.refs_0_), channel_id=1, source_target_pairs={{0,16},{16,0},{1,17},{17,1},{2,18},{18,2},{3,19},{19,3},{4,20},{20... | collective-permute-start | bytes 786440 | tf_op jit(solution)/shard_map/ppermute | solution.py:513
  60.2 6.2 %collective-permute-start.18 = (bf16[1,256,512]{2,1,0:T(8,128)(2,1)}, bf16[1,256,512]{2,1,0:T(8,128)(2,1)S(1)}, u32[]{:S(2)}, u32[]{:S(2)}) collective-permute-start(bf16[1,256,512]{2,1,0:T(8,128)(2,1)} %get-tuple-element.68.refs_1_), channel_id=1, source_target_pairs={{0,16},{16,0},{1,17},{17,1},{2,18},{18,2},{3,19},{19,3},{4,20},{20... | collective-permute-start | bytes 786440 | tf_op jit(solution)/shard_map/ppermute | solution.py:513
  60.3 6.1 %collective-permute-start.19 = (bf16[1,256,512]{2,1,0:T(8,128)(2,1)}, bf16[1,256,512]{2,1,0:T(8,128)(2,1)S(1)}, u32[]{:S(2)}, u32[]{:S(2)}) collective-permute-start(bf16[1,256,512]{2,1,0:T(8,128)(2,1)} %get-tuple-element.69.refs_2_), channel_id=1, source_target_pairs={{0,16},{16,0},{1,17},{17,1},{2,18},{18,2},{3,19},{19,3},{4,20},{20... | collective-permute-start | bytes 786440 | tf_op jit(solution)/shard_map/ppermute | solution.py:513
  63.2 3.3 %copy-start.9 = (bf16[1,2048,256]{2,1,0:T(8,128)(2,1)}, bf16[1,2048,256]{2,1,0:T(8,128)(2,1)S(1)}, u32[]{:S(2)}) copy-start(bf16[1,2048,256]{2,1,0:T(8,128)(2,1)S(1)} %collective-permute-done.2.refs_8_.refs_3_) | copy-start | bytes 3145732
  63.2 27.3 %collective-permute-start.5 = (bf16[1,2048,256]{2,1,0:T(8,128)(2,1)}, bf16[1,2048,256]{2,1,0:T(8,128)(2,1)}, u32[]{:S(2)}, u32[]{:S(2)}) collective-permute-start(bf16[1,2048,256]{2,1,0:T(8,128)(2,1)} %collective-permute-done.1.refs_4_.refs_2_), channel_id=1, source_target_pairs={{0,4},{4,8},{8,12},{12,0},{1,5},{5,9},{9,13},{13,1},{2,6},{6,10},{... | collective-permute-start | bytes 3145736 | tf_op jit(solution)/shard_map/ppermute | solution.py:513
  63.2 3.3 %copy-start.5 = (bf16[1,256,512]{2,1,0:T(8,128)(2,1)}, bf16[1,256,512]{2,1,0:T(8,128)(2,1)S(1)}, u32[]{:S(2)}) copy-start(bf16[1,256,512]{2,1,0:T(8,128)(2,1)S(1)} %collective-permute-done.17.refs_3_) | copy-start | bytes 786436
  63.2 27.3 %collective-permute-start.6 = (bf16[1,2048,256]{2,1,0:T(8,128)(2,1)}, bf16[1,2048,256]{2,1,0:T(8,128)(2,1)}, u32[]{:S(2)}, u32[]{:S(2)}) collective-permute-start(bf16[1,2048,256]{2,1,0:T(8,128)(2,1)} %collective-permute-done.4.refs_9_.refs_5_), channel_id=1, source_target_pairs={{0,12},{4,0},{8,4},{12,8},{1,13},{5,1},{9,5},{13,9},{2,14},{6,2},{... | collective-permute-start | bytes 3145736 | tf_op jit(solution)/shard_map/ppermute | solution.py:513
  66.5 0.7 copy-start.6
  66.5 0.8 copy-start.7
  66.5 1.0 copy-start.17
  72.0 28.2 %all-to-all-start = ((bf16[4,256,512]{2,1,0:T(8,128)(2,1)}), bf16[4,256,512]{2,1,0:T(8,128)(2,1)}, u32[]{:S(2)}, u32[]{:S(2)}) async-start(bf16[4,256,512]{2,1,0:T(8,128)(2,1)} %get-tuple-element.72.p_ref), calls=%async_computation | async-start | bytes 2097152 | tf_op jit(solution)/shard_map/all_to_all | solution.py:558
  76.2 34.6 %collective-permute-start.21 = (bf16[4,3,256,512]{3,2,1,0:T(8,128)(2,1)}, bf16[4,3,256,512]{3,2,1,0:T(8,128)(2,1)S(1)}, u32[]{:S(2)}, u32[]{:S(2)}) collective-permute-start(bf16[4,3,256,512]{3,2,1,0:T(8,128)(2,1)} %get-tuple-element.74.refs_6_), channel_id=1, source_target_pairs={{0,16},{16,0},{1,17},{17,1},{2,18},{18,2},{3,19},{19,3},{4,20},{20... | collective-permute-start | bytes 9437192 | tf_op jit(solution)/shard_map/ppermute | solution.py:513
  76.3 34.5 %collective-permute-start.22 = (bf16[3,3,256,512]{3,2,1,0:T(8,128)(2,1)}, bf16[3,3,256,512]{3,2,1,0:T(8,128)(2,1)}, u32[]{:S(2)}, u32[]{:S(2)}) collective-permute-start(bf16[3,3,256,512]{3,2,1,0:T(8,128)(2,1)} %get-tuple-element.75.refs_8_), channel_id=1, source_target_pairs={{0,16},{16,0},{1,17},{17,1},{2,18},{18,2},{3,19},{19,3},{4,20},{20... | collective-permute-start | bytes 7077896 | tf_op jit(solution)/shard_map/ppermute | solution.py:513
  106.4 4.4 %collective-permute-start.20 = (bf16[4,256,384]{2,1,0:T(8,128)(2,1)}, bf16[4,256,384]{2,1,0:T(8,128)(2,1)}, u32[]{:S(2)}, u32[]{:S(2)}) collective-permute-start(bf16[4,256,384]{2,1,0:T(8,128)(2,1)} %bitcast.18), channel_id=1, source_target_pairs={{0,16},{16,0},{1,17},{17,1},{2,18},{18,2},{3,19},{19,3},{4,20},{20... | collective-permute-start | bytes 2359304 | tf_op jit(solution)/shard_map/ppermute | solution.py:513
  106.4 17.5 %all-to-all-start.2 = ((bf16[4,256,384]{2,1,0:T(8,128)(2,1)}), bf16[4,256,384]{2,1,0:T(8,128)(2,1)}, u32[]{:S(2)}, u32[]{:S(2)}) async-start(bf16[4,256,384]{2,1,0:T(8,128)(2,1)} %bitcast.19), calls=%async_computation.2 | async-start | bytes 1572864 | tf_op jit(solution)/shard_map/all_to_all | solution.py:569
  110.8 1.6 copy-start
  123.9 25.8 %all-to-all-start.1 = ((bf16[4,512,384]{2,1,0:T(8,128)(2,1)}), bf16[4,512,384]{2,1,0:T(8,128)(2,1)S(1)}, u32[]{:S(2)}, u32[]{:S(2)}) async-start(bf16[4,512,384]{2,1,0:T(8,128)(2,1)} %bitcast.16), calls=%async_computation.1 | async-start | bytes 3145728 | tf_op jit(solution)/shard_map/all_to_all | solution.py:588
  136.2 18.0 %collective-permute-start.24 = (bf16[528,256]{1,0:T(8,128)(2,1)}, bf16[528,256]{1,0:T(8,128)(2,1)S(1)}, u32[]{:S(2)}, u32[]{:S(2)}) collective-permute-start(bf16[528,256]{1,0:T(8,128)(2,1)} %get-tuple-element.81), channel_id=1, source_target_pairs={{0,1},{1,2},{2,3},{3,0},{4,5},{5,6},{6,7},{7,4},{8,9},{9,10},{10,1... | collective-permute-start | bytes 811016 | tf_op jit(solution)/shard_map/ppermute | solution.py:513
  139.6 14.7 %collective-permute-start.25 = (bf16[512,256]{1,0:T(8,128)(2,1)}, bf16[512,256]{1,0:T(8,128)(2,1)S(1)}, u32[]{:S(2)}, u32[]{:S(2)}) collective-permute-start(bf16[512,256]{1,0:T(8,128)(2,1)} %get-tuple-element.84), channel_id=1, source_target_pairs={{0,3},{1,0},{2,1},{3,2},{4,7},{5,4},{6,5},{7,6},{8,11},{9,8},{10,9... | collective-permute-start | bytes 786440 | tf_op jit(solution)/shard_map/ppermute | solution.py:513
  149.6 1.1 copy-start.4
  153.1 5.9 %collective-permute-start.23 = (bf16[256,384]{1,0:T(8,128)(2,1)}, bf16[256,384]{1,0:T(8,128)(2,1)S(1)}, u32[]{:S(2)}, u32[]{:S(2)}) collective-permute-start(bf16[256,384]{1,0:T(8,128)(2,1)} %get-tuple-element.79), channel_id=1, source_target_pairs={{0,32},{32,0},{1,33},{33,1},{2,34},{34,2},{3,35},{35,3},{4,36},{36... | collective-permute-start | bytes 589832 | tf_op jit(solution)/shard_map/ppermute | solution.py:513
  154.2 4.8 %copy-start.18 = (bf16[512,256]{1,0:T(8,128)(2,1)}, bf16[512,256]{1,0:T(8,128)(2,1)S(1)}, u32[]{:S(2)}) copy-start(bf16[512,256]{1,0:T(8,128)(2,1)S(1)} %collective-permute-done.25.down_in) | copy-start | bytes 786436
  154.2 4.7 %copy-start.15 = (bf16[528,256]{1,0:T(8,128)(2,1)}, bf16[528,256]{1,0:T(8,128)(2,1)S(1)}, u32[]{:S(2)}) copy-start(bf16[528,256]{1,0:T(8,128)(2,1)S(1)} %collective-permute-done.24.up_in.stat_in) | copy-start | bytes 811012
  159.0 0.7 copy-start.16
  162.3 24.3 %collective-permute-start.27 = (bf16[1040,256]{1,0:T(8,128)(2,1)}, bf16[1040,256]{1,0:T(8,128)(2,1)S(1)}, u32[]{:S(2)}, u32[]{:S(2)}) collective-permute-start(bf16[1040,256]{1,0:T(8,128)(2,1)} %get-tuple-element.90), channel_id=1, source_target_pairs={{0,3},{1,0},{2,1},{3,2},{4,7},{5,4},{6,5},{7,6},{8,11},{9,8},{10,9... | collective-permute-start | bytes 1597448 | tf_op jit(solution)/shard_map/ppermute | solution.py:513
  167.7 24.2 %collective-permute-start.26 = (bf16[1040,256]{1,0:T(8,128)(2,1)}, bf16[1040,256]{1,0:T(8,128)(2,1)S(1)}, u32[]{:S(2)}, u32[]{:S(2)}) collective-permute-start(bf16[1040,256]{1,0:T(8,128)(2,1)} %get-tuple-element.86.refs_10_), channel_id=1, source_target_pairs={{0,1},{1,2},{2,3},{3,0},{4,5},{5,6},{6,7},{7,4},{8,9},{9,10},{10,1... | collective-permute-start | bytes 1597448 | tf_op jit(solution)/shard_map/ppermute | solution.py:513
  175.5 20.4 %all-to-all-start.3 = ((bf16[4,256,512]{2,1,0:T(8,128)(2,1)}), bf16[4,256,512]{2,1,0:T(8,128)(2,1)S(1)}, u32[]{:S(2)}, u32[]{:S(2)}) async-start(bf16[4,256,512]{2,1,0:T(8,128)(2,1)} %shard_map.73), calls=%async_computation.3 | async-start | bytes 2097152 | tf_op jit(solution)/shard_map/all_to_all | solution.py:598
  186.6 5.3 %copy-start.19 = (bf16[1040,256]{1,0:T(8,128)(2,1)}, bf16[1040,256]{1,0:T(8,128)(2,1)S(1)}, u32[]{:S(2)}) copy-start(bf16[1040,256]{1,0:T(8,128)(2,1)S(1)} %collective-permute-done.27.down) | copy-start | bytes 1597444
  191.9 0.8 copy-start.20
